TPU v7x, 512 devices: a whole 4x4x16 slice. The times are simulated.
512 devices in a mesh: ctx: 128 (over x, z, core), kvh: 4 (over y).
Axes of the slice: x: 4, y: 4, z: 16, core: 2. Of those that a mesh axis runs over, the one named last changes fastest.
Arguments:
- queries: bfloat16 [49152, 4096], P('ctx', 'kvh'), may hold values from -110 to 110
- keys: bfloat16 [49152, 1024], P('ctx', 'kvh'), may hold values from -4.5 to 4.5
- values: bfloat16 [49152, 1024], P('ctx', 'kvh'), may hold values from -6 to 6
- vertical: int32 [8, 4], P('kvh'), may hold values from 0 to 767, as said below
- offsets: int32 [8, 3], P('kvh'), may hold values from 0 to 319, as said below
Outputs:
- attended: bfloat16 [49152, 4096], P(('ctx', 'kvh'))
Inputs may be any that keep to these rules, and one draw needn't show every extreme that they name: `vertical`: each entry names a block of 64 keys; the 4 blocks of one key-value head lie in distinct shards of 384 positions. `offsets`: entry 0 of every head is 0; the bands [o, o + 64) of one head are disjoint.
All inputs are finite; a program needn't handle non-finite values.
Results may differ from a plain program's by a relative error of at most 0.0044.
Values may be sent and summed in bfloat16 or wider, within the bound.
No kernel may reach another device: no remote copies, remote signals or barrier semaphores. Data moves between devices by JAX's collectives and lax.ppermute only.
A program may use at most 128 MiB of HBM per device.

v0:
```python
import jax
import jax.numpy as jnp
from jax import lax
from jax.sharding import PartitionSpec as P

BLK = 64


NEG = -1e30


def shifted_2(shard, axis, by):
    devices = lax.axis_size(axis)
    pairs = [(i, i + by) for i in range(devices) if 0 <= i + by < devices]
    return lax.ppermute(shard, axis, pairs)


def band_tiles(window, begin, tok_rows, head_width):
    tile_count = tok_rows // BLK
    section = lax.dynamic_slice_in_dim(window, begin, tok_rows + BLK, 0)
    lower = section[:tok_rows].reshape(tile_count, BLK, head_width)
    upper = section[BLK:].reshape(tile_count, BLK, head_width)
    return jnp.concatenate([lower, upper], axis=1)


def attend(
    query_tile,
    first_pos,
    key_window,
    value_window,
    vert_keys,
    vert_values,
    vert_blocks,
    band_starts,
):
    tok_rows, group_size, head_width = query_tile.shape
    tile_count = tok_rows // BLK
    scaling = head_width ** (-0.5)
    query_pos = first_pos + jnp.arange(tok_rows, dtype=jnp.int32)
    vert_pos = (vert_blocks[:, None] * BLK + jnp.arange(BLK, dtype=jnp.int32)[None, :]).reshape(-1)
    distance = query_pos[:, None] - vert_pos[None, :]
    allowed = distance >= 0
    band_count = band_starts.shape[0]
    for band_num in range(band_count):
        shifted = distance - band_starts[band_num]
        allowed = allowed & ~((shifted >= 0) & (shifted < BLK))
    vert_scores = (
        jnp.einsum("qgd,kd->gqk", query_tile, vert_keys, preferred_element_type=jnp.float32)
        * scaling
    )
    vert_scores = jnp.where(allowed[None], vert_scores, NEG)
    begins = tok_rows - band_starts - BLK
    slash_keys = jnp.stack(
        [band_tiles(key_window, begins[b], tok_rows, head_width) for b in range(band_count)]
    )
    slash_values = jnp.stack(
        [band_tiles(value_window, begins[b], tok_rows, head_width) for b in range(band_count)]
    )
    query_blocks = query_tile.reshape(tile_count, BLK, group_size, head_width)
    slash_scores = (
        jnp.einsum("tagd,stcd->gstac", query_blocks, slash_keys, preferred_element_type=jnp.float32)
        * scaling
    )
    lag_rows = (
        jnp.arange(BLK, dtype=jnp.int32)[:, None]
        + BLK
        - jnp.arange(2 * BLK, dtype=jnp.int32)[None, :]
    )
    key_pos = (
        query_pos.reshape(tile_count, BLK)[None, :, :, None]
        - band_starts[:, None, None, None]
        - lag_rows[None, None]
    )
    band_mask = (lag_rows >= 0)[None, None] & (lag_rows < BLK)[None, None] & (key_pos >= 0)
    slash_scores = jnp.where(band_mask[None], slash_scores, NEG)
    row_top = jnp.maximum(
        vert_scores.max(axis=-1), slash_scores.max(axis=(1, 4)).reshape(group_size, tok_rows)
    )
    vert_exp = jnp.exp(vert_scores - row_top[:, :, None])
    slash_exp = jnp.exp(
        slash_scores - row_top.reshape(group_size, tile_count, BLK)[:, None, :, :, None]
    )
    totals = vert_exp.sum(axis=-1) + slash_exp.sum(axis=(1, 4)).reshape(group_size, tok_rows)
    vert_weights = vert_exp.astype(jnp.bfloat16)
    slash_weights = slash_exp.astype(jnp.bfloat16)
    blended = jnp.einsum(
        "gqk,kd->qgd", vert_weights, vert_values, preferred_element_type=jnp.float32
    )
    blended = blended + jnp.einsum(
        "gstac,stcd->tagd", slash_weights, slash_values, preferred_element_type=jnp.float32
    ).reshape(tok_rows, group_size, head_width)
    result = blended / totals.T[:, :, None]
    return result.astype(jnp.bfloat16).reshape(tok_rows, group_size * head_width)


def per_device(queries, keys, values, vertical, offsets):
    tok_rows = queries.shape[0]
    kv_heads = vertical.shape[0]
    head_width = keys.shape[1] // kv_heads
    group_size = queries.shape[1] // keys.shape[1]
    block_count = vertical.shape[1]
    per_shard = tok_rows // BLK
    shard_place = lax.axis_index("ctx")
    first_pos = shard_place * tok_rows
    earlier = shifted_2((keys, values), "ctx", 1)
    window_keys = jnp.concatenate([earlier[0], keys], axis=0)
    window_values = jnp.concatenate([earlier[1], values], axis=0)
    kv_local = jnp.stack(
        [
            keys.reshape(tok_rows, kv_heads, head_width),
            values.reshape(tok_rows, kv_heads, head_width),
        ],
        axis=0,
    )
    kv_local = kv_local.transpose(2, 0, 1, 3)
    owners = vertical // per_shard
    inside = vertical % per_shard
    mine = owners == shard_place
    offset_row = jnp.sum(jnp.where(mine, inside, 0), axis=1) * BLK
    present = jnp.any(mine, axis=1)
    slots = []
    for head_num in range(kv_heads):
        block_piece = lax.dynamic_slice_in_dim(kv_local[head_num], offset_row[head_num], BLK, 1)
        slots.append(jnp.where(present[head_num], block_piece, jnp.zeros_like(block_piece)))
    buffer = jnp.stack(slots)[None]
    gathered = lax.all_gather(buffer, "ctx", axis=0, tiled=True)
    fetched = []
    for head_num in range(kv_heads):
        picked = jnp.take(gathered[:, head_num], owners[head_num], axis=0)
        fetched.append(picked.transpose(1, 0, 2, 3).reshape(2, block_count * BLK, head_width))
    stored = jnp.stack(fetched)
    outputs = []
    query_heads = queries.reshape(tok_rows, kv_heads, group_size, head_width)
    for head_num in range(kv_heads):
        low = head_num * head_width
        outputs.append(
            attend(
                query_heads[:, head_num],
                first_pos,
                window_keys[:, low : low + head_width],
                window_values[:, low : low + head_width],
                stored[head_num, 0],
                stored[head_num, 1],
                vertical[head_num],
                offsets[head_num],
            )
        )
    joined = jnp.concatenate(outputs, axis=1)
    return lax.all_to_all(joined, "kvh", split_axis=0, concat_axis=1, tiled=True)


def solution(mesh):
    placed = (P("ctx", "kvh"), P("ctx", "kvh"), P("ctx", "kvh"), P("kvh", None), P("kvh", None))
    return jax.shard_map(
        per_device, mesh=mesh, in_specs=placed, out_specs=P(("ctx", "kvh"), None), check_vma=False
    )
```

profile of v0, /device:TPU:1, one launch (start us, length us, event | category | flops | bytes accessed | tf_op | source)
XLA Modules:
  0.0 253.8 jit_solution(5776707268589219783)
XLA Ops:
  6.5 0.9 fusion.98
  7.4 0.8 fusion.89
  12.1 1.2 copy.89
  13.2 1.1 copy.90
  15.7 1.4 dynamic-slice_select_fusion
  17.9 5.0 %collective-permute-start = (bf16[384,256]{1,0:T(8,128)(2,1)S(1)}, bf16[384,256]{1,0:T(8,128)(2,1)S(1)}, u32[]{:S(2)}, u32[]{:S(2)}) collective-permute-start(bf16[384,256]{1,0:T(8,128)(2,1)S(1)} %copy-done.4), channel_id=1, source_target_pairs={{0,4},{4,8},{8,12},{12,16},{16,20},{20,24},{24,28},{28,32},{32,36}... | collective-permute-start | bytes 589832 | tf_op jit(solution)/shard_map/ppermute | solution.py:15
  22.8 1.9 collective-permute-start.1
  38.5 4.4 %fusion.81 = (pred[384,256]{0,1:T(8,128)(4,1)S(1)}, pred[384,256]{0,1:T(8,128)(4,1)S(1)}) fusion(s32[]{:T(128)} %bitcast.17, s32[]{:T(128)} %bitcast.16, s32[]{:T(128)} %bitcast.15, s32[256]{0:T(256)S(1)} %add.143, s32[384]{0:T(512)S(1)} %iota_add_fusion.2, s32[]{:T(128)} %bitcast.67, s32[]{:T(128)} %bitcast.66, s32[]{:T(128)} %bitcast.65, s32[256]{0:T(256)S(1)} %add.155), kind=kLoop, calls=%fused_computation.107 | loop fusion | flops 3932160 | bytes 200216 | tf_op jit(solution)/shard_map/and | solution.py:46
  43.9 2.0 fusion.5
  46.3 2.0 fusion.4
  49.0 0.9 constant_dynamic-update-slice_fusion.3
  50.2 0.7 maximum_bitcast_fusion.8
  51.6 0.7 maximum_bitcast_fusion.9
  52.4 0.7 maximum_bitcast_fusion.14
  53.1 0.7 maximum_bitcast_fusion.16
  53.8 0.7 maximum_bitcast_fusion.15
  54.5 127.7 %all-gather.3.cloned.1.call-done = bf16[256,2,64,128]{2,3,0,1:T(8,128)(2,1)} async-done(((bf16[2,2,64,128]{2,3,0,1:T(8,128)(2,1)}), bf16[256,2,64,128]{2,3,0,1:T(8,128)(2,1)}) %all-gather.3.cloned.1.call-update) | async-done | bytes 8388624 | tf_op jit(solution)/shard_map/all_gather | solution.py:126
  182.1 15.9 %copy.91 = bf16[256,2,64,128]{3,2,1,0:T(8,128)(2,1)} copy(bf16[256,2,64,128]{2,3,0,1:T(8,128)(2,1)} %all-gather.3.cloned.1.call-done) | data formatting | bytes 16777216 | tf_op jit(solution)/shard_map/all_gather | solution.py:126
  198.0 8.0 %slice_bitcast_fusion.1 = (bf16[128,2,64,128]{3,2,1,0:T(8,128)(2,1)}, bf16[128,2,64,128]{3,2,1,0:T(8,128)(2,1)}) fusion(bf16[128,2,2,64,128]{4,3,2,1,0:T(8,128)(2,1)} %bitcast.229), kind=kLoop, calls=%fused_computation.3 | loop fusion | bytes 16777216 | tf_op jit(solution)/shard_map/squeeze | solution.py:129
  206.0 2.8 %gather_fusion = bf16[4,2,64,128]{3,2,1,0:T(8,128)(2,1)S(1)} fusion(bf16[128,2,64,128]{3,2,1,0:T(8,128)(2,1)} %get-tuple-element.12, s32[1024]{0:T(1024)S(1)} %get-tuple-element.90), kind=kCustom, calls=%fused_computation.clone | custom fusion | bytes 262160 | tf_op jit(solution)/shard_map/jit(_take)/gather | solution.py:129
  208.9 2.8 %gather_fusion.1 = bf16[4,2,64,128]{3,2,1,0:T(8,128)(2,1)S(1)} fusion(bf16[128,2,64,128]{3,2,1,0:T(8,128)(2,1)} %get-tuple-element.13, s32[1024]{0:T(1024)S(1)} %get-tuple-element.89), kind=kCustom, calls=%fused_computation.1.clone | custom fusion | bytes 262160 | tf_op jit(solution)/shard_map/jit(_take)/gather | solution.py:129
  212.9 2.5 fusion.2
  215.5 1.6 convolution_bitcast_fusion
  217.2 1.2 copy.114
  218.4 1.0 fusion.8
  219.5 1.9 fusion.14
  221.4 1.2 copy.116
  223.9 2.5 fusion
  226.5 1.6 convolution_bitcast_fusion.1
  228.5 0.9 fusion.6
  230.4 15.5 %all_to_all.16 = bf16[4,96,1024]{2,1,0:T(8,128)(2,1)S(1)} all-to-all(bf16[4,96,1024]{2,1,0:T(8,128)(2,1)S(1)} %pad_maximum_fusion), channel_id=1, replica_groups=mesh['ctx'=128,'kvh'=4] {'kvh'}, dimensions={0} | all-to-all | bytes 1572864 | tf_op jit(solution)/shard_map/all_to_all | solution.py:149
  246.0 0.9 copy.138
  (117 shorter events, 12.0 us)
Async XLA Ops:
  6.5 11.3 %copy-start.4 = (bf16[384,256]{1,0:T(8,128)(2,1)S(1)}, bf16[384,256]{1,0:T(8,128)(2,1)}, u32[]{:S(2)}) copy-start(bf16[384,256]{1,0:T(8,128)(2,1)} %param.8) | copy-start | bytes 589828
  6.5 16.3 %copy-start.5 = (bf16[384,256]{1,0:T(8,128)(2,1)S(1)}, bf16[384,256]{1,0:T(8,128)(2,1)}, u32[]{:S(2)}) copy-start(bf16[384,256]{1,0:T(8,128)(2,1)} %param.9) | copy-start | bytes 589828
  6.5 18.2 %copy-start.16 = (s32[2,3]{1,0:T(2,128)S(1)}, s32[2,3]{1,0:T(2,128)}, u32[]{:S(2)}) copy-start(s32[2,3]{1,0:T(2,128)} %param.11) | copy-start | bytes 76
  6.5 175.6 %all-gather.3.cloned.1.call-start = ((), (), s32[]{:S(2)}) async-start(), calls=%async_computation.1 | async-start | bytes 16908288 | tf_op jit(solution)/shard_map/all_gather | solution.py:126
  12.1 24.3 %copy-start.19 = (s32[2,4]{1,0:T(2,128)S(1)}, s32[2,4]{1,0:T(2,128)}, u32[]{:S(2)}) copy-start(s32[2,4]{1,0:T(2,128)} %param.10) | copy-start | bytes 100
  12.1 24.6 %copy-start.2 = (bf16[384,1024]{1,0:T(8,128)(2,1)S(1)}, bf16[384,1024]{1,0:T(8,128)(2,1)}, u32[]{:S(2)}) copy-start(bf16[384,1024]{1,0:T(8,128)(2,1)} %param.7) | copy-start | bytes 2359300
  17.9 25.7 %collective-permute-start = (bf16[384,256]{1,0:T(8,128)(2,1)S(1)}, bf16[384,256]{1,0:T(8,128)(2,1)S(1)}, u32[]{:S(2)}, u32[]{:S(2)}) collective-permute-start(bf16[384,256]{1,0:T(8,128)(2,1)S(1)} %copy-done.4), channel_id=1, source_target_pairs={{0,4},{4,8},{8,12},{12,16},{16,20},{20,24},{24,28},{28,32},{32,36}... | collective-permute-start | bytes 589832 | tf_op jit(solution)/shard_map/ppermute | solution.py:15
  22.8 26.2 %collective-permute-start.1 = (bf16[384,256]{1,0:T(8,128)(2,1)S(1)}, bf16[384,256]{1,0:T(8,128)(2,1)}, u32[]{:S(2)}, u32[]{:S(2)}) collective-permute-start(bf16[384,256]{1,0:T(8,128)(2,1)S(1)} %copy-done.5), channel_id=1, source_target_pairs={{0,4},{4,8},{8,12},{12,16},{16,20},{20,24},{24,28},{28,32},{32,36}... | collective-permute-start | bytes 589832 | tf_op jit(solution)/shard_map/ppermute | solution.py:15
  48.3 1.7 copy-start.14
  208.9 13.9 %copy-start.6 = (bf16[2,4,64,128]{3,2,1,0:T(8,128)(2,1)}, bf16[2,4,64,128]{3,2,1,0:T(8,128)(2,1)S(1)}, u32[]{:S(2)}) copy-start(bf16[2,4,64,128]{3,2,1,0:T(8,128)(2,1)S(1)} %copy.92) | copy-start | bytes 393220
  211.8 3.7 %copy-start.8 = (bf16[2,4,64,128]{3,2,1,0:T(8,128)(2,1)}, bf16[2,4,64,128]{3,2,1,0:T(8,128)(2,1)S(1)}, u32[]{:S(2)}) copy-start(bf16[2,4,64,128]{3,2,1,0:T(8,128)(2,1)S(1)} %copy.105) | copy-start | bytes 393220
  211.8 3.7 %copy-start.13 = (bf16[1,6,128,128]{3,2,0,1:T(8,128)(2,1)S(1)}, bf16[1,6,128,128]{3,2,0,1:T(8,128)(2,1)}, u32[]{:S(2)}) copy-start(bf16[1,6,128,128]{3,2,0,1:T(8,128)(2,1)} %maximum_bitcast_fusion.16) | copy-start | bytes 589828
  212.2 3.3 %copy-start.12 = (bf16[1,6,128,128]{3,2,0,1:T(8,128)(2,1)S(1)}, bf16[1,6,128,128]{3,2,0,1:T(8,128)(2,1)}, u32[]{:S(2)}) copy-start(bf16[1,6,128,128]{3,2,0,1:T(8,128)(2,1)} %maximum_bitcast_fusion.14) | copy-start | bytes 589828
  212.3 3.2 %copy-start.1 = (f32[6,3,128,64,4]{2,3,4,1,0:T(8,128)S(1)}, f32[6,3,128,64,4]{2,3,4,1,0:T(8,128)}, u32[]{:S(2)}) copy-start(f32[6,3,128,64,4]{2,3,4,1,0:T(8,128)} %get-tuple-element.77) | copy-start | bytes 7077892
  218.3 1.1 copy-start.3
  218.4 1.1 copy-start.9
  222.6 0.7 copy-start.18
  222.6 1.3 copy-start.15
  222.8 3.6 %copy-start.11 = (bf16[1,6,128,128]{3,2,0,1:T(8,128)(2,1)S(1)}, bf16[1,6,128,128]{3,2,0,1:T(8,128)(2,1)}, u32[]{:S(2)}) copy-start(bf16[1,6,128,128]{3,2,0,1:T(8,128)(2,1)} %maximum_bitcast_fusion.10) | copy-start | bytes 589828
  223.2 3.2 %copy-start.10 = (bf16[1,6,128,128]{3,2,0,1:T(8,128)(2,1)S(1)}, bf16[1,6,128,128]{3,2,0,1:T(8,128)(2,1)}, u32[]{:S(2)}) copy-start(bf16[1,6,128,128]{3,2,0,1:T(8,128)(2,1)} %maximum_bitcast_fusion.8) | copy-start | bytes 589828
  223.3 3.2 %copy-start = (f32[6,3,128,64,4]{2,3,4,1,0:T(8,128)S(1)}, f32[6,3,128,64,4]{2,3,4,1,0:T(8,128)}, u32[]{:S(2)}) copy-start(f32[6,3,128,64,4]{2,3,4,1,0:T(8,128)} %get-tuple-element.81) | copy-start | bytes 7077892
  228.4 1.0 copy-start.7
  228.4 1.0 copy-start.17
Sparse Core Ops, SparseCore 0:
  18.0 164.1 all-gather.2
where the time goes:
time: 255 us; the launch traced here: 254 us
  waiting for transfers between devices  128 us (50%)
  local copies, waits for them, and re-layouts  42.7 us (17%)
  between operations  28.8 us (11%)
  other arithmetic  21.9 us (9%)
  blocking collectives  15.5 us (6%)
  matrix products  10.4 us (4%)
  starting transfers between devices  6.89 us (3%)
    all_gather x1, waiting for transfers between devices, per_device(): gathered = lax.all_gather(buffer, 'ctx', axis=0, tiled=True)  128 us
    all_gather x1, local copies, waits for them, and re-layouts, per_device(): gathered = lax.all_gather(buffer, 'ctx', axis=0, tiled=True)  15.9 us
    all_to_all x1, blocking collectives, per_device(): lax.all_to_all(joined, 'kvh', split_axis=0, concat_axis=1, tiled=True)  15.5 us
    squeeze x1, local copies, waits for them, and re-layouts, per_device(): picked = jnp.take(gathered[:, head_num], owners[head_num], axis=0)  7.97 us
    ppermute x2, starting transfers between devices, shifted_2(): return lax.ppermute(shard, axis, pairs)  6.89 us
    gather x2, local copies, waits for them, and re-layouts, per_device(): picked = jnp.take(gathered[:, head_num], owners[head_num], axis=0)  5.56 us
  transfers between devices with their start and end apart: 3, of which 1 were waited for; matrix products, arithmetic and copies ran while one was open for 7% of the time, Pallas kernels for 0%

commit v1 on v0

v1 whole, which is shorter than its diff:
```python
import functools

import jax
import jax.numpy as jnp
from jax import lax
from jax.experimental import pallas as pl
from jax.experimental.pallas import tpu as pltpu
from jax.sharding import PartitionSpec as P

BLK = 64
ROWS = 48
TILE = 16
NEG = -1e30
LOG2E = 1.4426950408889634

N_X, N_FAR, N_NEAR, N_CORE = 4, 8, 2, 2
N_CLOSE = N_X * N_NEAR * N_CORE


def ctx_of(x, far, near, core):
    return ((x * N_FAR + far) * N_NEAR + near) * N_CORE + core


CLOSE_GROUPS = [
    [ctx_of(x, far, near, core) for x in range(N_X) for near in range(N_NEAR) for core in range(N_CORE)]
    for far in range(N_FAR)
]
FAR_GROUPS = [
    [ctx_of(x, far, near, core) for far in range(N_FAR)]
    for x in range(N_X)
    for near in range(N_NEAR)
    for core in range(N_CORE)
]


def close_far(block, per_shard):
    owner = lax.div(block, per_shard)
    core = lax.rem(owner, N_CORE)
    near = lax.rem(lax.div(owner, N_CORE), N_NEAR)
    far = lax.rem(lax.div(owner, N_CORE * N_NEAR), N_FAR)
    x = lax.div(owner, N_CORE * N_NEAR * N_FAR)
    return (x * N_NEAR + near) * N_CORE + core, far


def pack_kernel(place_ref, vert_ref, k_ref, v_ref, chunk_ref, both_ref):
    tok_rows = k_ref.shape[0]
    kv_heads, block_count = vert_ref.shape
    width = k_ref.shape[1] // kv_heads
    per_shard = tok_rows // BLK
    place = place_ref[0]
    for head in range(kv_heads):
        inside = jnp.int32(0)
        for j in range(block_count):
            block = vert_ref[head, j]
            mine = lax.div(block, per_shard) == place
            inside = inside + jnp.where(mine, lax.rem(block, per_shard), 0)
        rows = pl.ds(pl.multiple_of(inside * BLK, BLK), BLK)
        cols = slice(head * width, (head + 1) * width)
        chunk_ref[2 * head * BLK : (2 * head + 1) * BLK, :] = k_ref[rows, cols]
        chunk_ref[(2 * head + 1) * BLK : (2 * head + 2) * BLK, :] = v_ref[rows, cols]
    both_ref[:tok_rows, :] = k_ref[...]
    both_ref[tok_rows:, :] = v_ref[...]


def near_pick_kernel(place_ref, vert_ref, got_ref, out_ref, *, per_shard):
    kv_heads, block_count = vert_ref.shape
    x = lax.div(place_ref[0], N_CORE * N_NEAR * N_FAR)
    head = lax.div(x * kv_heads, N_X)
    for j in range(block_count):
        close, _ = close_far(vert_ref[head, j], per_shard)
        piece = got_ref[pl.ds(pl.multiple_of(close * TILE, TILE), TILE), :]
        for copy in range(N_FAR):
            low = (copy * block_count + j) * TILE
            out_ref[low : low + TILE, :] = piece


def far_pick_kernel(place_ref, vert_ref, got_ref, out_ref, *, per_shard):
    kv_heads, block_count = vert_ref.shape
    x = lax.div(place_ref[0], N_CORE * N_NEAR * N_FAR)
    head = lax.div(x * kv_heads, N_X)
    for j in range(block_count):
        _, far = close_far(vert_ref[head, j], per_shard)
        start = (far * block_count + j) * TILE
        piece = got_ref[pl.ds(pl.multiple_of(start, TILE), TILE), :]
        for copy in range(N_CLOSE):
            low = (copy * block_count + j) * TILE
            out_ref[low : low + TILE, :] = piece


def attend_kernel(
    place_ref, vert_ref, off_ref, q_ref, k_ref, v_ref, halo_ref, far_ref, out_ref, kwin, vwin
):
    tok_rows = k_ref.shape[0]
    kv_heads, block_count = vert_ref.shape
    band_count = off_ref.shape[1]
    width = k_ref.shape[1] // kv_heads
    group = q_ref.shape[1] // k_ref.shape[1]
    vert_rows = block_count * BLK
    slab = 128
    factor = width ** (-0.5) * LOG2E

    kwin[:tok_rows, :] = halo_ref[:tok_rows, :]
    vwin[:tok_rows, :] = halo_ref[tok_rows:, :]
    kwin[tok_rows : 2 * tok_rows, :] = k_ref[...]
    vwin[tok_rows : 2 * tok_rows, :] = v_ref[...]
    pad = kwin.shape[0] - 2 * tok_rows
    kwin[2 * tok_rows :, :] = jnp.zeros((pad, kwin.shape[1]), kwin.dtype)
    vwin[2 * tok_rows :, :] = jnp.zeros((pad, vwin.shape[1]), vwin.dtype)

    first_pos = place_ref[0] * tok_rows
    row = lax.broadcasted_iota(jnp.int32, (ROWS, slab), 0)
    col = lax.broadcasted_iota(jnp.int32, (ROWS, slab), 1)
    vert_row = lax.broadcasted_iota(jnp.int32, (ROWS, vert_rows), 0)
    vert_col = lax.broadcasted_iota(jnp.int32, (ROWS, vert_rows), 1)
    strip = (vert_col // TILE) % block_count
    inner = (vert_col // (block_count * TILE)) * TILE + vert_col % TILE

    bases, bands, lags = [], [], []
    for head in range(kv_heads):
        lag = vert_row - inner
        for j in range(block_count):
            lag = jnp.where(strip == j, lag - vert_ref[head, j] * BLK, lag)
        lags.append(lag)
        head_bases, head_bands = [], []
        for b in range(band_count):
            low = tok_rows - off_ref[head, b] - (BLK - 1)
            base = lax.div(low, TILE) * TILE
            shift = row - col + (tok_rows - off_ref[head, b] - base)
            head_bands.append((shift >= 0) & (shift < BLK))
            head_bases.append(base)
        bases.append(head_bases)
        bands.append(head_bands)

    def step(tile, carry):
        low = pl.multiple_of(tile * ROWS, TILE)
        for head in range(kv_heads):
            cols = slice(head * width, (head + 1) * width)
            query = jnp.concatenate(
                [
                    q_ref[pl.ds(low, ROWS), (head * group + i) * width : (head * group + i + 1) * width]
                    for i in range(group)
                ],
                axis=0,
            )
            key_parts, value_parts, masks = [], [], []
            for b in range(band_count):
                start = pl.multiple_of(bases[head][b] + low, TILE)
                key_parts.append(kwin[pl.ds(start, slab), cols])
                value_parts.append(vwin[pl.ds(start, slab), cols])
                masks.append(bands[head][b] & (col >= tok_rows - first_pos - start))
            vert_low = 2 * head * vert_rows
            key_parts.append(far_ref[vert_low : vert_low + vert_rows, :])
            value_parts.append(far_ref[vert_low + vert_rows : vert_low + 2 * vert_rows, :])
            distance = lags[head] + (first_pos + low)
            allowed = distance >= 0
            for b in range(band_count):
                shift = distance - off_ref[head, b]
                allowed = allowed & ((shift < 0) | (shift >= BLK))
            masks.append(allowed)

            scores = []
            top = None
            for keys, mask in zip(key_parts, masks):
                score = lax.dot_general(
                    query, keys, (((1,), (1,)), ((), ())), preferred_element_type=jnp.float32
                ).reshape(group, ROWS, keys.shape[0])
                score = jnp.where(mask[None], score, NEG)
                scores.append(score)
                part = score.max(axis=-1, keepdims=True)
                top = part if top is None else jnp.maximum(top, part)
            total = None
            weights = []
            for score in scores:
                weight = jnp.exp2((score - top) * factor)
                part = weight.sum(axis=-1, keepdims=True)
                total = part if total is None else total + part
                weights.append(
                    weight.astype(jnp.bfloat16).reshape(group * ROWS, score.shape[-1])
                )
            mixed = jnp.dot(
                jnp.concatenate(weights, axis=1),
                jnp.concatenate(value_parts, axis=0),
                preferred_element_type=jnp.float32,
            )
            mixed = mixed.reshape(group, ROWS, width) / total
            for i in range(group):
                left = (head * group + i) * width
                out_ref[pl.ds(low, ROWS), left : left + width] = mixed[i].astype(out_ref.dtype)
        return carry

    lax.fori_loop(0, tok_rows // ROWS, step, 0)


SMEM = pl.BlockSpec(memory_space=pltpu.SMEM)
VMEM = pl.BlockSpec(memory_space=pltpu.VMEM)


def call(kernel, out_shape, scalars, arrays, scratch=(), flops=0, transcendentals=0):
    shapes = out_shape if isinstance(out_shape, tuple) else (out_shape,)
    moved = sum(a.size * a.dtype.itemsize for a in arrays) + sum(s.size * 2 for s in shapes)
    return pl.pallas_call(
        kernel,
        out_shape=out_shape,
        in_specs=[SMEM] * len(scalars) + [VMEM] * len(arrays),
        out_specs=tuple(VMEM for _ in shapes) if isinstance(out_shape, tuple) else VMEM,
        scratch_shapes=list(scratch),
        compiler_params=pltpu.CompilerParams(vmem_limit_bytes=32 * 1024 * 1024),
        cost_estimate=pl.CostEstimate(
            flops=flops, bytes_accessed=moved, transcendentals=transcendentals
        ),
    )(*scalars, *arrays)


def per_device(queries, keys, values, vertical, offsets):
    tok_rows = queries.shape[0]
    kv_heads, block_count = vertical.shape
    width = keys.shape[1] // kv_heads
    per_shard = tok_rows // BLK
    place = lax.axis_index("ctx").astype(jnp.int32).reshape(1)
    brief = jax.ShapeDtypeStruct

    chunk, both = call(
        pack_kernel,
        (
            brief((2 * kv_heads * BLK, width), keys.dtype),
            brief((2 * tok_rows, keys.shape[1]), keys.dtype),
        ),
        (place, vertical),
        (keys, values),
    )
    devices = lax.axis_size("ctx")
    halo = lax.ppermute(both, "ctx", [(i, i + 1) for i in range(devices - 1)])

    strips = block_count * TILE
    got = lax.all_to_all(
        chunk, "ctx", split_axis=0, concat_axis=0, tiled=True, axis_index_groups=CLOSE_GROUPS
    )
    sent = call(
        functools.partial(near_pick_kernel, per_shard=per_shard),
        brief((N_FAR * strips, width), keys.dtype),
        (place, vertical),
        (got,),
    )
    got = lax.all_to_all(
        sent, "ctx", split_axis=0, concat_axis=0, tiled=True, axis_index_groups=FAR_GROUPS
    )
    sent = call(
        functools.partial(far_pick_kernel, per_shard=per_shard),
        brief((N_CLOSE * strips, width), keys.dtype),
        (place, vertical),
        (got,),
    )
    far = lax.all_to_all(
        sent, "ctx", split_axis=0, concat_axis=0, tiled=True, axis_index_groups=CLOSE_GROUPS
    )
    window = (2 * tok_rows + TILE, keys.shape[1])
    pairs = tok_rows * (queries.shape[1] // width) * (block_count * BLK + offsets.shape[1] * 128)
    joined = call(
        attend_kernel,
        brief(queries.shape, queries.dtype),
        (place, vertical, offsets),
        (queries, keys, values, halo, far),
        scratch=(pltpu.VMEM(window, keys.dtype), pltpu.VMEM(window, keys.dtype)),
        flops=4 * pairs * width,
        transcendentals=pairs,
    )
    return lax.all_to_all(joined, "kvh", split_axis=0, concat_axis=1, tiled=True)


def solution(mesh):
    placed = (P("ctx", "kvh"), P("ctx", "kvh"), P("ctx", "kvh"), P("kvh", None), P("kvh", None))
    return jax.shard_map(
        per_device, mesh=mesh, in_specs=placed, out_specs=P(("ctx", "kvh"), None), check_vma=False
    )
```

time: 255 us -> 85.3 us (0.33)
  waiting for transfers between devices: 128 us -> 4.7 us
  blocking collectives: 15.5 us -> 56.2 us
  local copies, waits for them, and re-layouts: 42.7 us -> 3.49 us
  between operations: 28.8 us -> 0.07 us
  other arithmetic: 21.9 us -> 0 us
  matrix products: 10.4 us -> 0 us
  Pallas kernels: 0 us -> 10.2 us
  starting transfers between devices: 6.89 us -> 10.3 us
    all_gather x1 -> x0, waiting for transfers between devices: 128 us -> none  [per_device(): gathered = lax.all_gather(buffer, 'ctx', axis=0, tiled=True)]
    all_to_all x0 -> x2, blocking collectives: none -> 40.1 us  [the longest x1 24.8 us: per_device(): lax.all_to_all(sent, 'ctx', split_axis=0, concat_axis=0, tiled=True, axis...]
    all_gather x1 -> x0, local copies, waits for them, and re-layouts: 15.9 us -> none  [per_device(): gathered = lax.all_gather(buffer, 'ctx', axis=0, tiled=True)]
    dot_general x8 -> x0, matrix products: 10.4 us -> none  [the longest x2 4.05 us: attend(): jnp.einsum('tagd,stcd->gstac', query_blocks, slash_keys, preferred_elemen...]
    pallas_call x0 -> x4, Pallas kernels: none -> 10.2 us  [call(): pl.pallas_call(kernel, out_shape=out_shape, in_specs=[SMEM] * len(scalars...]
    squeeze x1 -> x0, local copies, waits for them, and re-layouts: 7.97 us -> none  [per_device(): picked = jnp.take(gathered[:, head_num], owners[head_num], axis=0)]
    reduce_sum x5 -> x0, other arithmetic: 7.76 us -> none  [the longest x2 5.06 us: attend(): slash_exp.sum(axis=(1, 4)).reshape(group_size, tok_rows)]
    all_to_all x0 -> x1, starting transfers between devices: none -> 6.72 us  [per_device(): lax.all_to_all(sent, 'ctx', split_axis=0, concat_axis=0, tiled=True, axis...]
  transfers between devices with their start and end apart: 3 -> 2, of which waited for: 1 -> 1; matrix products, arithmetic and copies ran while one was open for 7% -> 0% of each run, Pallas kernels for 0% -> 0%
where the time goes in v1:
time: 85.3 us; the launch traced here: 84.9 us
  blocking collectives  56.2 us (66%)
  starting transfers between devices  10.3 us (12%)
  Pallas kernels  10.2 us (12%)
  waiting for transfers between devices  4.7 us (6%)
  local copies, waits for them, and re-layouts  3.49 us (4%)
    all_to_all x1, blocking collectives, per_device(): lax.all_to_all(sent, 'ctx', split_axis=0, concat_axis=0, tiled=True, axis...  24.8 us
    all_to_all x1, blocking collectives, per_device(): lax.all_to_all(joined, 'kvh', split_axis=0, concat_axis=1, tiled=True)  16.1 us
    all_to_all x1, blocking collectives, per_device(): lax.all_to_all(chunk, 'ctx', split_axis=0, concat_axis=0, tiled=True, axi...  15.3 us
    pallas_call x4, Pallas kernels, call(): pl.pallas_call(kernel, out_shape=out_shape, in_specs=[SMEM] * len(scalars...  10.2 us
    all_to_all x1, starting transfers between devices, per_device(): lax.all_to_all(sent, 'ctx', split_axis=0, concat_axis=0, tiled=True, axis...  6.72 us
    ppermute x1, waiting for transfers between devices, per_device(): halo = lax.ppermute(both, 'ctx', [(i, i + 1) for i in range(devices - 1)])  4.7 us
    ppermute x1, starting transfers between devices, per_device(): halo = lax.ppermute(both, 'ctx', [(i, i + 1) for i in range(devices - 1)])  3.55 us
    unnamed x14, local copies, waits for them, and re-layouts  2.55 us
  transfers between devices with their start and end apart: 2, of which 1 were waited for; matrix products, arithmetic and copies ran while one was open for 0% of the time, Pallas kernels for 0%

profile of v1, /device:TPU:1, one launch (start us, length us, event | category | flops | bytes accessed | tf_op | source)
XLA Modules:
  0.0 84.9 jit_solution(8388843177231332153)
XLA Ops:
  0.0 0.0 copy-start.4
  0.0 0.7 copy-done.4
  0.7 0.0 copy-start
  0.7 0.9 %copy-done = bf16[384,256]{1,0:T(8,128)(2,1)S(1)} copy-done((bf16[384,256]{1,0:T(8,128)(2,1)S(1)}, bf16[384,256]{1,0:T(8,128)(2,1)}, u32[]{:S(2)}) %copy-start) | copy-done | bytes 196632
  1.6 0.0 copy-start.2
  1.6 0.9 %copy-done.2 = bf16[384,256]{1,0:T(8,128)(2,1)S(1)} copy-done((bf16[384,256]{1,0:T(8,128)(2,1)S(1)}, bf16[384,256]{1,0:T(8,128)(2,1)}, u32[]{:S(2)}) %copy-start.2) | copy-done | bytes 196632
  2.5 0.6 shard_map.55
  3.1 0.0 copy-start.5
  3.1 15.3 %all_to_all.52 = bf16[16,16,128]{2,1,0:T(8,128)(2,1)S(1)} all-to-all(bf16[16,16,128]{2,1,0:T(8,128)(2,1)S(1)} %bitcast.16), channel_id=1, replica_groups={{0,4,8,12,128,132,136,140,256,260,264,268,384,388,392,396},{16,20,24,28..., dimensions={0} | all-to-all | bytes 131072 | tf_op jit(solution)/shard_map/all_to_all | solution.py:235
  18.4 0.6 shard_map.56
  19.0 24.8 %all_to_all.53 = bf16[8,64,128]{2,1,0:T(8,128)(2,1)S(1)} all-to-all(bf16[8,64,128]{2,1,0:T(8,128)(2,1)S(1)} %bitcast.12), channel_id=1, replica_groups={{0,16,32,48,64,80,96,112},{4,20,36,52,68,84,100,116},{8,24,40,56,72,88,..., dimensions={0} | all-to-all | bytes 262144 | tf_op jit(solution)/shard_map/all_to_all | solution.py:244
  43.8 1.3 %shard_map.57 = bf16[1024,128]{1,0:T(8,128)(2,1)} custom-call(s32[1]{0:T(128)} %bitcast.place_ref, s32[2,4]{1,0:T(2,128)S(1)} %copy-done.4, bf16[512,128]{1,0:T(8,128)(2,1)S(1)} %bitcast.13), custom_call_target="tpu_custom_call" | custom-call | bytes 393216 | tf_op jit(solution)/shard_map/pallas_call | solution.py:201
  45.1 0.0 copy-start.1
  45.1 0.0 copy-start.3
  45.1 6.7 %all-to-all-start.2 = ((bf16[16,64,128]{2,1,0:T(8,128)(2,1)}), bf16[16,64,128]{2,1,0:T(8,128)(2,1)S(1)}, u32[]{:S(2)}, u32[]{:S(2)}) async-start(bf16[16,64,128]{2,1,0:T(8,128)(2,1)} %bitcast.5), calls=%async_computation.2 | async-start | bytes 524288 | tf_op jit(solution)/shard_map/all_to_all | solution.py:253
  51.9 0.0 copy-start.6
  51.9 3.5 %collective-permute-start = (bf16[768,256]{1,0:T(8,128)(2,1)S(1)}, bf16[768,256]{1,0:T(8,128)(2,1)S(1)}, u32[]{:S(2)}, u32[]{:S(2)}) collective-permute-start(bf16[768,256]{1,0:T(8,128)(2,1)S(1)} %get-tuple-element.7), channel_id=1, source_target_pairs={{0,4},{4,8},{8,12},{12,16},{16,20},{20,24},{24,28},{28,32},{32,36}... | collective-permute-start | bytes 1179656 | tf_op jit(solution)/shard_map/ppermute | solution.py:232
  55.4 4.7 %collective-permute-done.halo_ref = bf16[768,256]{1,0:T(8,128)(2,1)S(1)} collective-permute-done((bf16[768,256]{1,0:T(8,128)(2,1)S(1)}, bf16[768,256]{1,0:T(8,128)(2,1)S(1)}, u32[]{:S(2)}, u32[]{:S(2)}) %collective-permute-start) | collective-permute-done | bytes 393248 | tf_op jit(solution)/shard_map/ppermute | solution.py:232
  60.1 0.0 all-to-all-done.2
  60.1 0.0 copy-done.5
  60.1 0.0 copy-done.1
  60.1 0.0 copy-done.3
  60.1 0.0 copy-done.6
  60.1 7.7 %shard_map.58 = bf16[384,1024]{1,0:T(8,128)(2,1)S(1)} custom-call(s32[1]{0:T(128)} %bitcast.place_ref, s32[2,4]{1,0:T(2,128)S(1)} %copy-done.4, s32[2,3]{1,0:T(2,128)S(1)} %copy-done.6, bf16[384,1024]{1,0:T(8,128)(2,1)S(1)} %copy-done.5, bf16[384,256]{1,0:T(8,128)(2,1)S(1)} %copy-done.1, bf16[384,256]{1,0:T(8,128)(2,1)S(1)} %copy-done.3, ...), custom_call_target="tpu_custom_call" | custom-call | flops 1006632960 | bytes 2621440 | tf_op jit(solution)/shard_map/pallas_call | solution.py:201
  67.8 16.1 %all_to_all.54 = bf16[4,96,1024]{2,1,0:T(8,128)(2,1)S(1)} all-to-all(bf16[4,96,1024]{2,1,0:T(8,128)(2,1)S(1)} %bitcast.11), channel_id=1, replica_groups=mesh['ctx'=128,'kvh'=4] {'kvh'}, dimensions={0} | all-to-all | bytes 1572864 | tf_op jit(solution)/shard_map/all_to_all | solution.py:267
  83.9 0.9 %copy.7 = bf16[4,12,8,1024]{3,2,0,1:T(8,128)(2,1)} copy(bf16[4,12,8,1024]{3,2,1,0:T(8,128)(2,1)S(1)} %bitcast.17) | data formatting | bytes 1572864 | tf_op jit(solution)/shard_map/all_to_all | solution.py:267
Async XLA Ops:
  0.0 0.7 copy-start.4
  0.7 0.9 %copy-start = (bf16[384,256]{1,0:T(8,128)(2,1)S(1)}, bf16[384,256]{1,0:T(8,128)(2,1)}, u32[]{:S(2)}) copy-start(bf16[384,256]{1,0:T(8,128)(2,1)} %k_ref.3) | copy-start | bytes 589828
  1.6 0.9 %copy-start.2 = (bf16[384,256]{1,0:T(8,128)(2,1)S(1)}, bf16[384,256]{1,0:T(8,128)(2,1)}, u32[]{:S(2)}) copy-start(bf16[384,256]{1,0:T(8,128)(2,1)} %v_ref.3) | copy-start | bytes 589828
  3.1 57.0 %copy-start.5 = (bf16[384,1024]{1,0:T(8,128)(2,1)S(1)}, bf16[384,1024]{1,0:T(8,128)(2,1)}, u32[]{:S(2)}) copy-start(bf16[384,1024]{1,0:T(8,128)(2,1)} %q_ref.1) | copy-start | bytes 2359300
  45.1 15.0 %copy-start.1 = (bf16[384,256]{1,0:T(8,128)(2,1)S(1)}, bf16[384,256]{1,0:T(8,128)(2,1)}, u32[]{:S(2)}) copy-start(bf16[384,256]{1,0:T(8,128)(2,1)} %k_ref.3) | copy-start | bytes 589828
  45.1 15.0 %copy-start.3 = (bf16[384,256]{1,0:T(8,128)(2,1)S(1)}, bf16[384,256]{1,0:T(8,128)(2,1)}, u32[]{:S(2)}) copy-start(bf16[384,256]{1,0:T(8,128)(2,1)} %v_ref.3) | copy-start | bytes 589828
  45.1 15.0 %all-to-all-start.2 = ((bf16[16,64,128]{2,1,0:T(8,128)(2,1)}), bf16[16,64,128]{2,1,0:T(8,128)(2,1)S(1)}, u32[]{:S(2)}, u32[]{:S(2)}) async-start(bf16[16,64,128]{2,1,0:T(8,128)(2,1)} %bitcast.5), calls=%async_computation.2 | async-start | bytes 524288 | tf_op jit(solution)/shard_map/all_to_all | solution.py:253
  51.9 8.3 %copy-start.6 = (s32[2,3]{1,0:T(2,128)S(1)}, s32[2,3]{1,0:T(2,128)}, u32[]{:S(2)}) copy-start(s32[2,3]{1,0:T(2,128)} %off_ref.1) | copy-start | bytes 76
  51.9 8.3 %collective-permute-start = (bf16[768,256]{1,0:T(8,128)(2,1)S(1)}, bf16[768,256]{1,0:T(8,128)(2,1)S(1)}, u32[]{:S(2)}, u32[]{:S(2)}) collective-permute-start(bf16[768,256]{1,0:T(8,128)(2,1)S(1)} %get-tuple-element.7), channel_id=1, source_target_pairs={{0,4},{4,8},{8,12},{12,16},{16,20},{20,24},{24,28},{28,32},{32,36}... | collective-permute-start | bytes 1179656 | tf_op jit(solution)/shard_map/ppermute | solution.py:232

commit v2 on v1

v2 whole, which is shorter than its diff:
```python
import functools

import jax
import jax.numpy as jnp
from jax import lax
from jax.experimental import pallas as pl
from jax.experimental.pallas import tpu as pltpu
from jax.sharding import PartitionSpec as P

BLK = 64
TILE = 16
LANES = 128
SLASH_ROWS = 48
VERT_ROWS = 2 * SLASH_ROWS
NEG = -1e30
LOG2E = 1.4426950408889634

N_X, N_FAR, N_NEAR, N_CORE = 4, 8, 2, 2
N_CLOSE = N_X * N_NEAR * N_CORE


def ctx_of(x, far, near, core):
    return ((x * N_FAR + far) * N_NEAR + near) * N_CORE + core


CLOSE_GROUPS = [
    [ctx_of(x, far, near, core) for x in range(N_X) for near in range(N_NEAR) for core in range(N_CORE)]
    for far in range(N_FAR)
]
FAR_GROUPS = [
    [ctx_of(x, far, near, core) for far in range(N_FAR)]
    for x in range(N_X)
    for near in range(N_NEAR)
    for core in range(N_CORE)
]


def owner_of(block, per_shard):
    return (block * (65536 // per_shard + 1)) >> 16


def place_of(block, per_shard):
    owner = owner_of(block, per_shard)
    spread = N_NEAR * N_CORE
    far = (owner // spread) & (N_FAR - 1)
    x = owner // (spread * N_FAR)
    return x * spread + (owner & (spread - 1)), far


def pack_kernel(vert_hbm, k_hbm, v_hbm, chunk_ref, both_ref, vert_ref, sems):
    tok_rows = k_hbm.shape[0]
    kv_heads, block_count = vert_ref.shape
    width = k_hbm.shape[1] // kv_heads
    per_shard = tok_rows // BLK
    copies = [
        pltpu.make_async_copy(vert_hbm, vert_ref, sems.at[0]),
        pltpu.make_async_copy(k_hbm, both_ref.at[pl.ds(0, tok_rows)], sems.at[1]),
        pltpu.make_async_copy(v_hbm, both_ref.at[pl.ds(tok_rows, tok_rows)], sems.at[2]),
    ]
    for copy in copies:
        copy.start()
    place = lax.axis_index("ctx")
    copies[0].wait()
    starts = []
    for head in range(kv_heads):
        inside = jnp.int32(0)
        for j in range(block_count):
            block = vert_ref[head, j]
            owner = owner_of(block, per_shard)
            inside = inside + jnp.where(owner == place, block - owner * per_shard, 0)
        starts.append(inside * BLK)
    for part in range(2):
        copies[1 + part].wait()
        for head in range(kv_heads):
            rows = pl.ds(pl.multiple_of(part * tok_rows + starts[head], BLK), BLK)
            low = (2 * head + part) * BLK
            chunk_ref[low : low + BLK, :] = both_ref[rows, head * width : (head + 1) * width]


def near_pick_kernel(plan_ref, got_ref, out_ref):
    _, kv_heads, block_count = plan_ref.shape
    place = lax.axis_index("ctx")
    head = (place // (N_CORE * N_NEAR * N_FAR)) * kv_heads // N_X
    my_far = (place // (N_CORE * N_NEAR)) & (N_FAR - 1)
    for j in range(block_count):
        close = plan_ref[0, head, j]
        piece = got_ref[pl.ds(pl.multiple_of(close * TILE, TILE), TILE), :]
        piece = jnp.where(plan_ref[1, head, j] == my_far, piece, jnp.zeros_like(piece))
        for copy in range(N_FAR):
            low = (copy * block_count + j) * TILE
            out_ref[low : low + TILE, :] = piece


def far_pick_kernel(got_ref, out_ref):
    rows = got_ref.shape[0] // N_FAR
    total = got_ref[:rows, :]
    for source in range(1, N_FAR):
        total = total + got_ref[source * rows : (source + 1) * rows, :]
    for copy in range(N_CLOSE):
        out_ref[copy * rows : (copy + 1) * rows, :] = total


def stacked(ref, low, rows, head, group, width):
    return jnp.concatenate(
        [
            ref[pl.ds(low, rows), (head * group + i) * width : (head * group + i + 1) * width]
            for i in range(group)
        ],
        axis=0,
    )


def unstack(ref, low, rows, head, group, width, stack):
    for i in range(group):
        left = (head * group + i) * width
        ref[pl.ds(low, rows), left : left + width] = stack[i * rows : (i + 1) * rows].astype(ref.dtype)


def masked(score, mask, group):
    rows, cols = mask.shape
    score = jnp.where(mask[None], score.reshape(group, rows, cols), NEG)
    return score.reshape(group * rows, cols)


def across(reduce, combine, parts):
    return reduce(functools.reduce(combine, parts), axis=1, keepdims=True)


def lanes(score):
    return [score[:, c : c + LANES] for c in range(0, score.shape[1], LANES)]


def slash_kernel(
    off_ref, q_ref, k_ref, v_ref, halo_ref, mixed_ref, level_ref, kwin, vwin
):
    tok_rows = q_ref.shape[0]
    kv_heads, band_count = off_ref.shape
    width = k_ref.shape[1] // kv_heads
    group = q_ref.shape[1] // k_ref.shape[1]
    factor = width ** (-0.5) * LOG2E

    kwin[:tok_rows, :] = halo_ref[:tok_rows, :]
    vwin[:tok_rows, :] = halo_ref[tok_rows:, :]
    kwin[tok_rows : 2 * tok_rows, :] = k_ref[...]
    vwin[tok_rows : 2 * tok_rows, :] = v_ref[...]
    pad = kwin.shape[0] - 2 * tok_rows
    kwin[2 * tok_rows :, :] = jnp.zeros((pad, kwin.shape[1]), kwin.dtype)
    vwin[2 * tok_rows :, :] = jnp.zeros((pad, vwin.shape[1]), vwin.dtype)

    level_ref[...] = jnp.zeros_like(level_ref)
    first_pos = lax.axis_index("ctx") * tok_rows
    row = lax.broadcasted_iota(jnp.int32, (SLASH_ROWS, LANES), 0)
    col = lax.broadcasted_iota(jnp.int32, (SLASH_ROWS, LANES), 1)

    def step(tile, carry):
        low = pl.multiple_of(tile * SLASH_ROWS, TILE)
        scores, value_parts = [], []
        for head in range(kv_heads):
            cols = slice(head * width, (head + 1) * width)
            keys, values, masks = [], [], []
            for b in range(band_count):
                reach = tok_rows - off_ref[head, b] - (BLK - 1)
                base = lax.div(reach, TILE) * TILE
                start = pl.multiple_of(base + low, TILE)
                lag = row - col + (reach - base + BLK - 1)
                masks.append(((lag & -BLK) == 0) & (col >= tok_rows - first_pos - start))
                keys.append(kwin[pl.ds(start, LANES), cols])
                values.append(vwin[pl.ds(start, LANES), cols])
            score = lax.dot_general(
                stacked(q_ref, low, SLASH_ROWS, head, group, width),
                jnp.concatenate(keys, axis=0),
                (((1,), (1,)), ((), ())),
                preferred_element_type=jnp.float32,
            )
            scores.append([masked(p, m, group) for p, m in zip(lanes(score), masks)])
            value_parts.append(jnp.concatenate(values, axis=0))
        tops = [across(jnp.max, jnp.maximum, parts) for parts in scores]
        weights = [
            [jnp.exp2((part - top) * factor) for part in parts] for parts, top in zip(scores, tops)
        ]
        totals = [across(jnp.sum, jnp.add, parts) for parts in weights]
        levels = level_ref[...]
        for head in range(kv_heads):
            mixed = jnp.dot(
                jnp.concatenate([w.astype(jnp.bfloat16) for w in weights[head]], axis=1),
                value_parts[head],
                preferred_element_type=jnp.float32,
            )
            unstack(mixed_ref, low, SLASH_ROWS, head, group, width, mixed / totals[head])
            level = tops[head] * factor + jnp.log2(totals[head])
            for i in range(group):
                rows = slice(i * SLASH_ROWS, (i + 1) * SLASH_ROWS)
                spot = (tile * kv_heads + head) * group + i
                levels = jnp.where(col == spot, level[rows], levels)
        level_ref[...] = levels
        return carry

    lax.fori_loop(0, tok_rows // SLASH_ROWS, step, 0, unroll=4)


def vertical_kernel(
    vert_ref, off_ref, q_ref, far_ref, mixed_ref, level_ref, out_ref
):
    tok_rows = q_ref.shape[0]
    kv_heads, block_count = vert_ref.shape
    band_count = off_ref.shape[1]
    width = far_ref.shape[1]
    group = q_ref.shape[1] // (kv_heads * width)
    vert_rows = block_count * BLK
    factor = width ** (-0.5) * LOG2E
    first_pos = lax.axis_index("ctx") * tok_rows
    row = lax.broadcasted_iota(jnp.int32, (VERT_ROWS, LANES), 0)
    col = lax.broadcasted_iota(jnp.int32, (VERT_ROWS, LANES), 1)
    strip = (col // TILE) % block_count
    inner = (col // (block_count * TILE)) * TILE + col % TILE

    for tile in range(tok_rows // VERT_ROWS):
        low = tile * VERT_ROWS
        scores = []
        for head in range(kv_heads):
            vert_low = 2 * head * vert_rows
            score = lax.dot_general(
                stacked(q_ref, low, VERT_ROWS, head, group, width),
                far_ref[vert_low : vert_low + vert_rows, :],
                (((1,), (1,)), ((), ())),
                preferred_element_type=jnp.float32,
            )
            begin = jnp.zeros_like(strip)
            for j in range(block_count):
                begin = jnp.where(strip == j, vert_ref[head, j] * BLK, begin)
            parts = []
            for num, part in enumerate(lanes(score)):
                lag = row - inner - begin + (first_pos + low - num * (LANES // block_count))
                allowed = lag >= 0
                for b in range(band_count):
                    allowed = allowed & (((lag - off_ref[head, b]) & -BLK) != 0)
                parts.append(masked(part, allowed, group))
            scores.append(parts)
        spots = [(low, VERT_ROWS, head, group, width) for head in range(kv_heads)]
        levels = [
            jnp.concatenate(
                [
                    jnp.broadcast_to(level_ref[:, spot : spot + 1], (SLASH_ROWS, LANES))
                    for i in range(group)
                    for part in range(VERT_ROWS // SLASH_ROWS)
                    for spot in [((tile * VERT_ROWS // SLASH_ROWS + part) * kv_heads + head) * group + i]
                ],
                axis=0,
            )
            for head in range(kv_heads)
        ]
        tops = [
            jnp.maximum(across(jnp.max, jnp.maximum, parts) * factor, level)
            for parts, level in zip(scores, levels)
        ]
        weights = [
            [jnp.exp2(part * factor - top) for part in parts] for parts, top in zip(scores, tops)
        ]
        totals = [across(jnp.sum, jnp.add, parts) for parts in weights]
        for head, spot in enumerate(spots):
            vert_low = (2 * head + 1) * vert_rows
            mixed = jnp.dot(
                jnp.concatenate([w.astype(jnp.bfloat16) for w in weights[head]], axis=1),
                far_ref[vert_low : vert_low + vert_rows, :],
                preferred_element_type=jnp.float32,
            )
            fade = jnp.exp2(levels[head] - tops[head])
            mixed = mixed + stacked(mixed_ref, *spot) * fade
            unstack(out_ref, *spot, mixed / (totals[head] + fade))


SMEM = pl.BlockSpec(memory_space=pltpu.SMEM)
VMEM = pl.BlockSpec(memory_space=pltpu.VMEM)


VMEM_PACK = 60 * 1024 * 1024


def call(
    kernel,
    out_shape,
    scalars,
    arrays,
    scratch=(),
    flops=0,
    transcendentals=0,
    space=pltpu.VMEM,
    vmem=16 * 1024 * 1024,
):
    shapes = out_shape if isinstance(out_shape, tuple) else (out_shape,)
    moved = sum(a.size * a.dtype.itemsize for a in arrays + shapes)
    return pl.pallas_call(
        kernel,
        out_shape=out_shape,
        in_specs=[SMEM] * len(scalars) + [pl.BlockSpec(memory_space=space)] * len(arrays),
        out_specs=tuple(VMEM for _ in shapes) if isinstance(out_shape, tuple) else VMEM,
        scratch_shapes=list(scratch),
        compiler_params=pltpu.CompilerParams(vmem_limit_bytes=vmem),
        cost_estimate=pl.CostEstimate(
            flops=flops, bytes_accessed=moved, transcendentals=transcendentals
        ),
    )(*scalars, *arrays)


def per_device(queries, keys, values, vertical, offsets):
    tok_rows = queries.shape[0]
    kv_heads, block_count = vertical.shape
    width = keys.shape[1] // kv_heads
    heads = queries.shape[1] // width
    brief = jax.ShapeDtypeStruct
    chunk, both = call(
        pack_kernel,
        (
            brief((2 * kv_heads * BLK, width), keys.dtype),
            brief((2 * tok_rows, keys.shape[1]), keys.dtype),
        ),
        (),
        (vertical, keys, values),
        scratch=(pltpu.SMEM(vertical.shape, vertical.dtype), pltpu.SemaphoreType.DMA((3,))),
        space=pltpu.HBM,
        vmem=VMEM_PACK,
    )
    strips = block_count * TILE
    chunk, blocks = lax.optimization_barrier((chunk, vertical))
    plan = jnp.stack(place_of(blocks, tok_rows // BLK))
    got = lax.all_to_all(
        chunk, "ctx", split_axis=0, concat_axis=0, tiled=True, axis_index_groups=CLOSE_GROUPS
    )
    got, sent_back = lax.optimization_barrier((got, both))
    sent = call(
        near_pick_kernel,
        brief((N_FAR * strips, width), keys.dtype),
        (plan,),
        (got,),
    )
    devices = lax.axis_size("ctx")
    halo = lax.ppermute(sent_back, "ctx", [(i, i + 1) for i in range(devices - 1)])
    got = lax.all_to_all(
        sent, "ctx", split_axis=0, concat_axis=0, tiled=True, axis_index_groups=FAR_GROUPS
    )
    got, halo = lax.optimization_barrier((got, halo))
    sent = call(
        far_pick_kernel,
        brief((N_CLOSE * strips, width), keys.dtype),
        (),
        (got,),
    )
    far = lax.all_to_all(
        sent, "ctx", split_axis=0, concat_axis=0, tiled=True, axis_index_groups=CLOSE_GROUPS
    )
    window = (2 * tok_rows + TILE, keys.shape[1])
    slash_pairs = tok_rows * heads * offsets.shape[1] * LANES
    mixed, levels = call(
        slash_kernel,
        (brief(queries.shape, jnp.float32), brief((SLASH_ROWS, LANES), jnp.float32)),
        (offsets,),
        (queries, keys, values, halo),
        scratch=(pltpu.VMEM(window, keys.dtype), pltpu.VMEM(window, keys.dtype)),
        flops=4 * slash_pairs * width,
        transcendentals=slash_pairs,
    )
    vert_pairs = tok_rows * heads * block_count * BLK
    joined = call(
        vertical_kernel,
        brief(queries.shape, queries.dtype),
        (vertical, offsets),
        (queries, far, mixed, levels),
        flops=4 * vert_pairs * width,
        transcendentals=vert_pairs,
    )
    return lax.all_to_all(joined, "kvh", split_axis=0, concat_axis=1, tiled=True)


def solution(mesh):
    placed = (P("ctx", "kvh"), P("ctx", "kvh"), P("ctx", "kvh"), P("kvh", None), P("kvh", None))
    return jax.shard_map(
        per_device, mesh=mesh, in_specs=placed, out_specs=P(("ctx", "kvh"), None), check_vma=False
    )
```

time: 85.3 us -> 77.8 us (0.912)
  blocking collectives: 56.2 us -> 14.7 us
  starting transfers between devices: 10.3 us -> 30.8 us
  waiting for transfers between devices: 4.7 us -> 19.3 us
  local copies, waits for them, and re-layouts: 3.49 us -> 0.97 us
    all_to_all x2 -> x0, blocking collectives: 40.1 us -> none  [the longest x1 24.8 us: per_device(): lax.all_to_all(sent, 'ctx', split_axis=0, concat_axis=0, tiled=True, axis...]
    all_to_all x1 -> x2, starting transfers between devices: 6.72 us -> 17.7 us  [per_device(): lax.all_to_all(sent, 'ctx', split_axis=0, concat_axis=0, tiled=True, axis...]
    all_to_all x0 -> x1, starting transfers between devices: none -> 10.2 us  [per_device(): lax.all_to_all(chunk, 'ctx', split_axis=0, concat_axis=0, tiled=True, axi...]
    all_to_all x1 -> x2, waiting for transfers between devices: 0.01 us -> 5.38 us  [per_device(): lax.all_to_all(sent, 'ctx', split_axis=0, concat_axis=0, tiled=True, axis...]
    all_to_all x0 -> x1, waiting for transfers between devices: none -> 5.18 us  [per_device(): lax.all_to_all(chunk, 'ctx', split_axis=0, concat_axis=0, tiled=True, axi...]
    ppermute x1, waiting for transfers between devices: 4.7 us -> 8.72 us  [per_device(): lax.ppermute(sent_back, 'ctx', [(i, i + 1) for i in range(devices - 1)])]
    unnamed x14 -> x10, local copies, waits for them, and re-layouts: 2.55 us -> 0.02 us
    all_to_all x1, blocking collectives: 16.1 us -> 14.7 us  [per_device(): lax.all_to_all(joined, 'kvh', split_axis=0, concat_axis=1, tiled=True)]
  transfers between devices with their start and end apart: 2 -> 4, of which waited for: 1 -> 4; matrix products, arithmetic and copies ran while one was open for 0% -> 1% of each run, Pallas kernels for 0% -> 5%
where the time goes in v2:
time: 77.8 us; the launch traced here: 77 us
  starting transfers between devices  30.8 us (40%)
  waiting for transfers between devices  19.3 us (25%)
  blocking collectives  14.7 us (19%)
  Pallas kernels  10.4 us (13%)
  local copies, waits for them, and re-layouts  0.97 us (1%)
    all_to_all x2, starting transfers between devices, per_device(): lax.all_to_all(sent, 'ctx', split_axis=0, concat_axis=0, tiled=True, axis...  17.7 us
    all_to_all x1, blocking collectives, per_device(): lax.all_to_all(joined, 'kvh', split_axis=0, concat_axis=1, tiled=True)  14.7 us
    pallas_call x5, Pallas kernels, call(): pl.pallas_call(kernel, out_shape=out_shape, in_specs=[SMEM] * len(scalars...  10.4 us
    all_to_all x1, starting transfers between devices, per_device(): lax.all_to_all(chunk, 'ctx', split_axis=0, concat_axis=0, tiled=True, axi...  10.2 us
    ppermute x1, waiting for transfers between devices, per_device(): lax.ppermute(sent_back, 'ctx', [(i, i + 1) for i in range(devices - 1)])  8.72 us
    all_to_all x2, waiting for transfers between devices, per_device(): lax.all_to_all(sent, 'ctx', split_axis=0, concat_axis=0, tiled=True, axis...  5.38 us
    all_to_all x1, waiting for transfers between devices, per_device(): lax.all_to_all(chunk, 'ctx', split_axis=0, concat_axis=0, tiled=True, axi...  5.18 us
    ppermute x1, starting transfers between devices, per_device(): lax.ppermute(sent_back, 'ctx', [(i, i + 1) for i in range(devices - 1)])  2.87 us
  transfers between devices with their start and end apart: 4, of which 4 were waited for; matrix products, arithmetic and copies ran while one was open for 1% of the time, Pallas kernels for 5%

profile of v2, /device:TPU:1, one launch (start us, length us, event | category | flops | bytes accessed | tf_op | source)
XLA Modules:
  0.0 77.0 jit_solution(2255713990047780442)
XLA Ops:
  0.0 0.0 copy-start.2
  0.0 0.0 copy-start.1
  0.0 0.0 copy-start.4
  0.0 0.0 copy-start
  0.0 1.9 %shard_map.55 = (bf16[256,128]{1,0:T(8,128)(2,1)}, bf16[768,256]{1,0:T(8,128)(2,1)}) custom-call(s32[2,4]{1,0:T(2,128)} %vert_ref.1, bf16[384,256]{1,0:T(8,128)(2,1)} %k_ref.1, bf16[384,256]{1,0:T(8,128)(2,1)} %v_ref.1), custom_call_target="tpu_custom_call" | custom-call | bytes 852000 | tf_op jit(solution)/shard_map/pallas_call | solution.py:292
  1.9 10.2 %all-to-all-start = ((bf16[16,16,128]{2,1,0:T(8,128)(2,1)}), bf16[16,16,128]{2,1,0:T(8,128)(2,1)S(1)}, u32[]{:S(2)}, u32[]{:S(2)}) async-start(bf16[16,16,128]{2,1,0:T(8,128)(2,1)} %bitcast.19), calls=%async_computation | async-start | bytes 131072 | tf_op jit(solution)/shard_map/all_to_all | solution.py:326
  12.1 0.7 add_bitcast_fusion
  12.8 5.2 %all-to-all-done = bf16[16,16,128]{2,1,0:T(8,128)(2,1)S(1)} async-done(((bf16[16,16,128]{2,1,0:T(8,128)(2,1)}), bf16[16,16,128]{2,1,0:T(8,128)(2,1)S(1)}, u32[]{:S(2)}, u32[]{:S(2)}) %all-to-all-start) | async-done | bytes 65568 | tf_op jit(solution)/shard_map/all_to_all | solution.py:326
  18.0 1.3 %shard_map.56 = bf16[512,128]{1,0:T(8,128)(2,1)} custom-call(s32[2,2,4]{2,1,0:T(2,128)S(1)} %pad_add_fusion.plan_ref, bf16[256,128]{1,0:T(8,128)(2,1)S(1)} %bitcast.17), custom_call_target="tpu_custom_call" | custom-call | bytes 196608 | tf_op jit(solution)/shard_map/pallas_call | solution.py:292
  19.2 10.9 %all-to-all-start.1 = ((bf16[8,64,128]{2,1,0:T(8,128)(2,1)}), bf16[8,64,128]{2,1,0:T(8,128)(2,1)S(1)}, u32[]{:S(2)}, u32[]{:S(2)}) async-start(bf16[8,64,128]{2,1,0:T(8,128)(2,1)} %bitcast.4), calls=%async_computation.1 | async-start | bytes 262144 | tf_op jit(solution)/shard_map/all_to_all | solution.py:338
  30.1 2.9 %collective-permute-start = (bf16[768,256]{1,0:T(8,128)(2,1)}, bf16[768,256]{1,0:T(8,128)(2,1)S(1)}, u32[]{:S(2)}, u32[]{:S(2)}) collective-permute-start(bf16[768,256]{1,0:T(8,128)(2,1)} %get-tuple-element.20), channel_id=1, source_target_pairs={{0,4},{4,8},{8,12},{12,16},{16,20},{20,24},{24,28},{28,32},{32,36}... | collective-permute-start | bytes 1179656 | tf_op jit(solution)/shard_map/ppermute | solution.py:337
  33.0 8.7 %collective-permute-done.halo_ref = bf16[768,256]{1,0:T(8,128)(2,1)S(1)} collective-permute-done((bf16[768,256]{1,0:T(8,128)(2,1)}, bf16[768,256]{1,0:T(8,128)(2,1)S(1)}, u32[]{:S(2)}, u32[]{:S(2)}) %collective-permute-start) | collective-permute-done | bytes 393248 | tf_op jit(solution)/shard_map/ppermute | solution.py:337
  41.7 1.8 %all-to-all-done.1 = bf16[8,64,128]{2,1,0:T(8,128)(2,1)S(1)} async-done(((bf16[8,64,128]{2,1,0:T(8,128)(2,1)}), bf16[8,64,128]{2,1,0:T(8,128)(2,1)S(1)}, u32[]{:S(2)}, u32[]{:S(2)}) %all-to-all-start.1) | async-done | bytes 131104 | tf_op jit(solution)/shard_map/all_to_all | solution.py:338
  43.5 0.0 copy-start.3
  43.6 0.7 shard_map.57
  44.3 6.9 %all-to-all-start.2 = ((bf16[16,64,128]{2,1,0:T(8,128)(2,1)}), bf16[16,64,128]{2,1,0:T(8,128)(2,1)S(1)}, u32[]{:S(2)}, u32[]{:S(2)}) async-start(bf16[16,64,128]{2,1,0:T(8,128)(2,1)} %bitcast.6), calls=%async_computation.2 | async-start | bytes 524288 | tf_op jit(solution)/shard_map/all_to_all | solution.py:348
  51.2 0.0 copy-done.2
  51.2 0.0 copy-done.1
  51.2 0.0 copy-done.4
  51.2 0.0 copy-done
  51.2 3.7 %shard_map.58 = (f32[384,1024]{1,0:T(8,128)S(1)}, f32[48,128]{1,0:T(8,128)S(1)}) custom-call(s32[2,3]{1,0:T(2,128)S(1)} %copy-done.4, bf16[384,1024]{1,0:T(8,128)(2,1)S(1)} %copy-done, bf16[384,256]{1,0:T(8,128)(2,1)S(1)} %copy-done.1, bf16[384,256]{1,0:T(8,128)(2,1)S(1)} %copy-done.2, bf16[768,256]{1,0:T(8,128)(2,1)S(1)} %collective-permute-done.halo_ref), custom_call_target="tpu_custom_call" | custom-call | flops 603979776 | bytes 3170304 | tf_op jit(solution)/shard_map/pallas_call | solution.py:292
  54.9 3.5 %all-to-all-done.2 = bf16[16,64,128]{2,1,0:T(8,128)(2,1)S(1)} async-done(((bf16[16,64,128]{2,1,0:T(8,128)(2,1)}), bf16[16,64,128]{2,1,0:T(8,128)(2,1)S(1)}, u32[]{:S(2)}, u32[]{:S(2)}) %all-to-all-start.2) | async-done | bytes 262176 | tf_op jit(solution)/shard_map/all_to_all | solution.py:348
  58.4 0.0 copy-done.3
  58.4 2.9 %shard_map.59 = bf16[384,1024]{1,0:T(8,128)(2,1)S(1)} custom-call(s32[2,4]{1,0:T(2,128)S(1)} %copy-done.3, s32[2,3]{1,0:T(2,128)S(1)} %copy-done.4, bf16[384,1024]{1,0:T(8,128)(2,1)S(1)} %copy-done, bf16[1024,128]{1,0:T(8,128)(2,1)S(1)} %bitcast.15, f32[384,1024]{1,0:T(8,128)S(1)} %get-tuple-element.23.mixed_ref, f32[48,128]{1,0:T(8,128)S(1)} %get-tuple-element.24.level_ref), custom_call_target="tpu_custom_call" | custom-call | flops 402653184 | bytes 3432448 | tf_op jit(solution)/shard_map/pallas_call | solution.py:292
  61.3 14.7 %all_to_all.54 = bf16[4,96,1024]{2,1,0:T(8,128)(2,1)S(1)} all-to-all(bf16[4,96,1024]{2,1,0:T(8,128)(2,1)S(1)} %bitcast.14), channel_id=1, replica_groups=mesh['ctx'=128,'kvh'=4] {'kvh'}, dimensions={0} | all-to-all | bytes 1572864 | tf_op jit(solution)/shard_map/all_to_all | solution.py:371
  76.0 0.9 %copy.7 = bf16[4,12,8,1024]{3,2,0,1:T(8,128)(2,1)} copy(bf16[4,12,8,1024]{3,2,1,0:T(8,128)(2,1)S(1)} %bitcast.18) | data formatting | bytes 1572864 | tf_op jit(solution)/shard_map/all_to_all | solution.py:371
  (1 shorter events, 0.0 us)
Async XLA Ops:
  0.0 51.2 %copy-start.2 = (bf16[384,256]{1,0:T(8,128)(2,1)S(1)}, bf16[384,256]{1,0:T(8,128)(2,1)}, u32[]{:S(2)}) copy-start(bf16[384,256]{1,0:T(8,128)(2,1)} %v_ref.1) | copy-start | bytes 589828
  0.0 51.2 %copy-start.1 = (bf16[384,256]{1,0:T(8,128)(2,1)S(1)}, bf16[384,256]{1,0:T(8,128)(2,1)}, u32[]{:S(2)}) copy-start(bf16[384,256]{1,0:T(8,128)(2,1)} %k_ref.1) | copy-start | bytes 589828
  0.0 51.2 %copy-start.4 = (s32[2,3]{1,0:T(2,128)S(1)}, s32[2,3]{1,0:T(2,128)}, u32[]{:S(2)}) copy-start(s32[2,3]{1,0:T(2,128)} %off_ref.3) | copy-start | bytes 76
  0.0 51.2 %copy-start = (bf16[384,1024]{1,0:T(8,128)(2,1)S(1)}, bf16[384,1024]{1,0:T(8,128)(2,1)}, u32[]{:S(2)}) copy-start(bf16[384,1024]{1,0:T(8,128)(2,1)} %q_ref.3) | copy-start | bytes 2359300
  1.9 16.0 %all-to-all-start = ((bf16[16,16,128]{2,1,0:T(8,128)(2,1)}), bf16[16,16,128]{2,1,0:T(8,128)(2,1)S(1)}, u32[]{:S(2)}, u32[]{:S(2)}) async-start(bf16[16,16,128]{2,1,0:T(8,128)(2,1)} %bitcast.19), calls=%async_computation | async-start | bytes 131072 | tf_op jit(solution)/shard_map/all_to_all | solution.py:326
  19.2 24.3 %all-to-all-start.1 = ((bf16[8,64,128]{2,1,0:T(8,128)(2,1)}), bf16[8,64,128]{2,1,0:T(8,128)(2,1)S(1)}, u32[]{:S(2)}, u32[]{:S(2)}) async-start(bf16[8,64,128]{2,1,0:T(8,128)(2,1)} %bitcast.4), calls=%async_computation.1 | async-start | bytes 262144 | tf_op jit(solution)/shard_map/all_to_all | solution.py:338
  30.1 11.6 %collective-permute-start = (bf16[768,256]{1,0:T(8,128)(2,1)}, bf16[768,256]{1,0:T(8,128)(2,1)S(1)}, u32[]{:S(2)}, u32[]{:S(2)}) collective-permute-start(bf16[768,256]{1,0:T(8,128)(2,1)} %get-tuple-element.20), channel_id=1, source_target_pairs={{0,4},{4,8},{8,12},{12,16},{16,20},{20,24},{24,28},{28,32},{32,36}... | collective-permute-start | bytes 1179656 | tf_op jit(solution)/shard_map/ppermute | solution.py:337
  43.5 14.8 %copy-start.3 = (s32[2,4]{1,0:T(2,128)S(1)}, s32[2,4]{1,0:T(2,128)}, u32[]{:S(2)}) copy-start(s32[2,4]{1,0:T(2,128)} %vert_ref.1) | copy-start | bytes 100
  44.3 14.1 %all-to-all-start.2 = ((bf16[16,64,128]{2,1,0:T(8,128)(2,1)}), bf16[16,64,128]{2,1,0:T(8,128)(2,1)S(1)}, u32[]{:S(2)}, u32[]{:S(2)}) async-start(bf16[16,64,128]{2,1,0:T(8,128)(2,1)} %bitcast.6), calls=%async_computation.2 | async-start | bytes 524288 | tf_op jit(solution)/shard_map/all_to_all | solution.py:348

commit v3 on v2

--- a/solution.py
+++ b/solution.py
@@ -17,6 +17,11 @@
 
 N_X, N_FAR, N_NEAR, N_CORE = 4, 8, 2, 2
 N_CLOSE = N_X * N_NEAR * N_CORE
+SHIFT_FAR = (N_NEAR * N_CORE).bit_length() - 1
+SHIFT_X = (N_FAR * N_NEAR * N_CORE).bit_length() - 1
+SHIFT_HEAD = N_X.bit_length() - 1
+SHIFT_TILE = TILE.bit_length() - 1
+SHIFT_BLK = BLK.bit_length() - 1
 
 
 def ctx_of(x, far, near, core):
@@ -42,12 +47,12 @@
 def place_of(block, per_shard):
     owner = owner_of(block, per_shard)
     spread = N_NEAR * N_CORE
-    far = (owner // spread) & (N_FAR - 1)
-    x = owner // (spread * N_FAR)
+    far = (owner >> SHIFT_FAR) & (N_FAR - 1)
+    x = owner >> SHIFT_X
     return x * spread + (owner & (spread - 1)), far
 
 
-def pack_kernel(vert_hbm, k_hbm, v_hbm, chunk_ref, both_ref, vert_ref, sems):
+def pack_kernel(vert_hbm, k_hbm, v_hbm, chunk_ref, vert_ref, both_ref, sems):
     tok_rows = k_hbm.shape[0]
     kv_heads, block_count = vert_ref.shape
     width = k_hbm.shape[1] // kv_heads
@@ -77,18 +82,47 @@
             chunk_ref[low : low + BLK, :] = both_ref[rows, head * width : (head + 1) * width]
 
 
-def near_pick_kernel(plan_ref, got_ref, out_ref):
-    _, kv_heads, block_count = plan_ref.shape
+def prepare_kernel(vert_ref, k_ref, v_ref, choice_ref, both_ref):
+    kv_heads, block_count = vert_ref.shape
+    tok_rows = k_ref.shape[0]
+    per_shard = tok_rows // BLK
     place = lax.axis_index("ctx")
-    head = (place // (N_CORE * N_NEAR * N_FAR)) * kv_heads // N_X
-    my_far = (place // (N_CORE * N_NEAR)) & (N_FAR - 1)
+    head = ((place >> SHIFT_X) * kv_heads) >> SHIFT_HEAD
+    my_far = (place >> SHIFT_FAR) & (N_FAR - 1)
+    row = lax.broadcasted_iota(jnp.int32, (TILE, choice_ref.shape[1]), 0)
+    col = lax.broadcasted_iota(jnp.int32, (TILE, choice_ref.shape[1]), 1)
     for j in range(block_count):
-        close = plan_ref[0, head, j]
-        piece = got_ref[pl.ds(pl.multiple_of(close * TILE, TILE), TILE), :]
-        piece = jnp.where(plan_ref[1, head, j] == my_far, piece, jnp.zeros_like(piece))
-        for copy in range(N_FAR):
-            low = (copy * block_count + j) * TILE
-            out_ref[low : low + TILE, :] = piece
+        close, far = place_of(vert_ref[head, j], per_shard)
+        wanted = jnp.where(far == my_far, close * TILE, -2 * TILE) + row
+        choice_ref[j * TILE : (j + 1) * TILE, :] = jnp.where(col == wanted, 1.0, 0.0).astype(
+            choice_ref.dtype
+        )
+    both_ref[:tok_rows, :] = k_ref[...]
+    both_ref[tok_rows:, :] = v_ref[...]
+
+
+def key_places(vert_ref, off_ref, place_ref):
+    kv_heads, block_count = vert_ref.shape
+    band_count = off_ref.shape[1]
+    col = lax.broadcasted_iota(jnp.int32, (1, place_ref.shape[1]), 1)
+    strip = (col >> SHIFT_TILE) & (block_count - 1)
+    inner = (col >> SHIFT_BLK) * TILE + (col & (TILE - 1))
+    for head in range(kv_heads):
+        begin = jnp.zeros_like(col)
+        for j in range(block_count):
+            begin = jnp.where(strip == j, vert_ref[head, j] * BLK, begin)
+        place_ref[head : head + 1, :] = begin + inner
+        for b in range(band_count):
+            at = kv_heads + head * band_count + b
+            place_ref[at : at + 1, :] = jnp.full(col.shape, off_ref[head, b], jnp.int32)
+
+
+def near_pick_kernel(choice_ref, got_ref, out_ref):
+    pieces = jnp.dot(choice_ref[...], got_ref[...], preferred_element_type=jnp.float32)
+    pieces = pieces.astype(out_ref.dtype)
+    rows = pieces.shape[0]
+    for copy in range(N_FAR):
+        out_ref[copy * rows : (copy + 1) * rows, :] = pieces
 
 
 def far_pick_kernel(got_ref, out_ref):
@@ -131,7 +165,7 @@
 
 
 def slash_kernel(
-    off_ref, q_ref, k_ref, v_ref, halo_ref, mixed_ref, level_ref, kwin, vwin
+    vert_ref, off_ref, q_ref, k_ref, v_ref, halo_ref, mixed_ref, level_ref, place_ref, kwin, vwin
 ):
     tok_rows = q_ref.shape[0]
     kv_heads, band_count = off_ref.shape
@@ -148,6 +182,7 @@
     vwin[2 * tok_rows :, :] = jnp.zeros((pad, vwin.shape[1]), vwin.dtype)
 
     level_ref[...] = jnp.zeros_like(level_ref)
+    key_places(vert_ref, off_ref, place_ref)
     first_pos = lax.axis_index("ctx") * tok_rows
     row = lax.broadcasted_iota(jnp.int32, (SLASH_ROWS, LANES), 0)
     col = lax.broadcasted_iota(jnp.int32, (SLASH_ROWS, LANES), 1)
@@ -199,21 +234,16 @@
 
 
 def vertical_kernel(
-    vert_ref, off_ref, q_ref, far_ref, mixed_ref, level_ref, out_ref
+    place_ref, q_ref, far_ref, mixed_ref, level_ref, out_ref, *, kv_heads
 ):
     tok_rows = q_ref.shape[0]
-    kv_heads, block_count = vert_ref.shape
-    band_count = off_ref.shape[1]
+    band_count = place_ref.shape[0] // kv_heads - 1
     width = far_ref.shape[1]
     group = q_ref.shape[1] // (kv_heads * width)
-    vert_rows = block_count * BLK
+    vert_rows = far_ref.shape[0] // (2 * kv_heads)
     factor = width ** (-0.5) * LOG2E
     first_pos = lax.axis_index("ctx") * tok_rows
     row = lax.broadcasted_iota(jnp.int32, (VERT_ROWS, LANES), 0)
-    col = lax.broadcasted_iota(jnp.int32, (VERT_ROWS, LANES), 1)
-    strip = (col // TILE) % block_count
-    inner = (col // (block_count * TILE)) * TILE + col % TILE
-
     for tile in range(tok_rows // VERT_ROWS):
         low = tile * VERT_ROWS
         scores = []
@@ -225,15 +255,14 @@
                 (((1,), (1,)), ((), ())),
                 preferred_element_type=jnp.float32,
             )
-            begin = jnp.zeros_like(strip)
-            for j in range(block_count):
-                begin = jnp.where(strip == j, vert_ref[head, j] * BLK, begin)
             parts = []
             for num, part in enumerate(lanes(score)):
-                lag = row - inner - begin + (first_pos + low - num * (LANES // block_count))
+                cols = slice(num * LANES, (num + 1) * LANES)
+                lag = row + (first_pos + low) - place_ref[head : head + 1, cols]
                 allowed = lag >= 0
                 for b in range(band_count):
-                    allowed = allowed & (((lag - off_ref[head, b]) & -BLK) != 0)
+                    at = kv_heads + head * band_count + b
+                    allowed = allowed & (((lag - place_ref[at : at + 1, cols]) & -BLK) != 0)
                 parts.append(masked(part, allowed, group))
             scores.append(parts)
         spots = [(low, VERT_ROWS, head, group, width) for head in range(kv_heads)]
@@ -308,33 +337,42 @@
     width = keys.shape[1] // kv_heads
     heads = queries.shape[1] // width
     brief = jax.ShapeDtypeStruct
-    chunk, both = call(
+    chunk = call(
         pack_kernel,
+        brief((2 * kv_heads * BLK, width), keys.dtype),
+        (),
+        (vertical, keys, values),
+        scratch=(
+            pltpu.SMEM(vertical.shape, vertical.dtype),
+            pltpu.VMEM((2 * tok_rows, keys.shape[1]), keys.dtype),
+            pltpu.SemaphoreType.DMA((3,)),
+        ),
+        space=pltpu.HBM,
+        vmem=VMEM_PACK,
+    )
+    strips = block_count * TILE
+    chunk, blocks, own = lax.optimization_barrier((chunk, vertical, (keys, values)))
+    choice, both = call(
+        prepare_kernel,
         (
-            brief((2 * kv_heads * BLK, width), keys.dtype),
+            brief((strips, N_CLOSE * TILE), keys.dtype),
             brief((2 * tok_rows, keys.shape[1]), keys.dtype),
         ),
-        (),
-        (vertical, keys, values),
-        scratch=(pltpu.SMEM(vertical.shape, vertical.dtype), pltpu.SemaphoreType.DMA((3,))),
-        space=pltpu.HBM,
-        vmem=VMEM_PACK,
-    )
-    strips = block_count * TILE
-    chunk, blocks = lax.optimization_barrier((chunk, vertical))
-    plan = jnp.stack(place_of(blocks, tok_rows // BLK))
+        (blocks,),
+        own,
+    )
     got = lax.all_to_all(
         chunk, "ctx", split_axis=0, concat_axis=0, tiled=True, axis_index_groups=CLOSE_GROUPS
     )
-    got, sent_back = lax.optimization_barrier((got, both))
+    got, choice, both = lax.optimization_barrier((got, choice, both))
     sent = call(
         near_pick_kernel,
         brief((N_FAR * strips, width), keys.dtype),
-        (plan,),
-        (got,),
+        (),
+        (choice, got),
     )
     devices = lax.axis_size("ctx")
-    halo = lax.ppermute(sent_back, "ctx", [(i, i + 1) for i in range(devices - 1)])
+    halo = lax.ppermute(both, "ctx", [(i, i + 1) for i in range(devices - 1)])
     got = lax.all_to_all(
         sent, "ctx", split_axis=0, concat_axis=0, tiled=True, axis_index_groups=FAR_GROUPS
     )
@@ -350,10 +388,14 @@
     )
     window = (2 * tok_rows + TILE, keys.shape[1])
     slash_pairs = tok_rows * heads * offsets.shape[1] * LANES
-    mixed, levels = call(
+    mixed, levels, places = call(
         slash_kernel,
-        (brief(queries.shape, jnp.float32), brief((SLASH_ROWS, LANES), jnp.float32)),
-        (offsets,),
+        (
+            brief(queries.shape, jnp.float32),
+            brief((SLASH_ROWS, LANES), jnp.float32),
+            brief((kv_heads * (1 + offsets.shape[1]), block_count * BLK), jnp.int32),
+        ),
+        (vertical, offsets),
         (queries, keys, values, halo),
         scratch=(pltpu.VMEM(window, keys.dtype), pltpu.VMEM(window, keys.dtype)),
         flops=4 * slash_pairs * width,
@@ -361,10 +403,10 @@
     )
     vert_pairs = tok_rows * heads * block_count * BLK
     joined = call(
-        vertical_kernel,
+        functools.partial(vertical_kernel, kv_heads=kv_heads),
         brief(queries.shape, queries.dtype),
-        (vertical, offsets),
-        (queries, far, mixed, levels),
+        (),
+        (places, queries, far, mixed, levels),
         flops=4 * vert_pairs * width,
         transcendentals=vert_pairs,
     )

time: 77.8 us -> 76.8 us (0.987)
  local copies, waits for them, and re-layouts: 0.97 us -> 3.48 us
  waiting for transfers between devices: 19.3 us -> 16.8 us
    unnamed x10 -> x16, local copies, waits for them, and re-layouts: 0.02 us -> 2.54 us
    all_to_all x1, waiting for transfers between devices: 5.18 us -> 2.75 us  [per_device(): lax.all_to_all(chunk, 'ctx', split_axis=0, concat_axis=0, tiled=True, axi...]
    pallas_call x5 -> x6, Pallas kernels: 10.4 us -> 9.86 us  [call(): pl.pallas_call(kernel, out_shape=out_shape, in_specs=[SMEM] * len(scalars...]
  transfers between devices with their start and end apart: 4 -> 4, of which waited for: 4 -> 4; matrix products, arithmetic and copies ran while one was open for 1% -> 0% of each run, Pallas kernels for 5% -> 6%
where the time goes in v3:
time: 76.8 us; the launch traced here: 76 us
  starting transfers between devices  31 us (40%)
  waiting for transfers between devices  16.8 us (22%)
  blocking collectives  14.7 us (19%)
  Pallas kernels  9.86 us (13%)
  local copies, waits for them, and re-layouts  3.48 us (5%)
    all_to_all x2, starting transfers between devices, per_device(): lax.all_to_all(sent, 'ctx', split_axis=0, concat_axis=0, tiled=True, axis...  18 us
    all_to_all x1, blocking collectives, per_device(): lax.all_to_all(joined, 'kvh', split_axis=0, concat_axis=1, tiled=True)  14.7 us
    all_to_all x1, starting transfers between devices, per_device(): lax.all_to_all(chunk, 'ctx', split_axis=0, concat_axis=0, tiled=True, axi...  10.2 us
    pallas_call x6, Pallas kernels, call(): pl.pallas_call(kernel, out_shape=out_shape, in_specs=[SMEM] * len(scalars...  9.86 us
    ppermute x1, waiting for transfers between devices, per_device(): halo = lax.ppermute(both, 'ctx', [(i, i + 1) for i in range(devices - 1)])  8.61 us
    all_to_all x2, waiting for transfers between devices, per_device(): lax.all_to_all(sent, 'ctx', split_axis=0, concat_axis=0, tiled=True, axis...  5.47 us
    ppermute x1, starting transfers between devices, per_device(): halo = lax.ppermute(both, 'ctx', [(i, i + 1) for i in range(devices - 1)])  2.87 us
    all_to_all x1, waiting for transfers between devices, per_device(): lax.all_to_all(chunk, 'ctx', split_axis=0, concat_axis=0, tiled=True, axi...  2.75 us
  transfers between devices with their start and end apart: 4, of which 4 were waited for; matrix products, arithmetic and copies ran while one was open for 0% of the time, Pallas kernels for 6%

profile of v3, /device:TPU:1, one launch (start us, length us, event | category | flops | bytes accessed | tf_op | source)
XLA Modules:
  0.0 76.0 jit_solution(14123126338875875307)
XLA Ops:
  0.0 0.0 copy-start.6
  0.0 0.0 copy-start.3
  0.0 0.0 copy-start.1
  0.0 0.0 copy-start.7
  0.0 1.7 %shard_map.55 = bf16[256,128]{1,0:T(8,128)(2,1)} custom-call(s32[2,4]{1,0:T(2,128)} %vert_ref.2, bf16[384,256]{1,0:T(8,128)(2,1)} %k_ref.2, bf16[384,256]{1,0:T(8,128)(2,1)} %v_ref.2), custom_call_target="tpu_custom_call" | custom-call | bytes 458784 | tf_op jit(solution)/shard_map/pallas_call | solution.py:321
  1.8 10.2 %all-to-all-start = ((bf16[16,16,128]{2,1,0:T(8,128)(2,1)}), bf16[16,16,128]{2,1,0:T(8,128)(2,1)S(1)}, u32[]{:S(2)}, u32[]{:S(2)}) async-start(bf16[16,16,128]{2,1,0:T(8,128)(2,1)} %bitcast.15), calls=%async_computation | async-start | bytes 131072 | tf_op jit(solution)/shard_map/all_to_all | solution.py:364
  11.9 0.0 copy-start
  11.9 0.9 %copy-done = bf16[384,256]{1,0:T(8,128)(2,1)S(1)} copy-done((bf16[384,256]{1,0:T(8,128)(2,1)S(1)}, bf16[384,256]{1,0:T(8,128)(2,1)}, u32[]{:S(2)}) %copy-start) | copy-done | bytes 196632
  12.9 0.0 copy-start.2
  12.9 0.9 %copy-done.2 = bf16[384,256]{1,0:T(8,128)(2,1)S(1)} copy-done((bf16[384,256]{1,0:T(8,128)(2,1)S(1)}, bf16[384,256]{1,0:T(8,128)(2,1)}, u32[]{:S(2)}) %copy-start.2) | copy-done | bytes 196632
  13.8 0.0 copy-start.5
  13.8 0.7 copy-done.5
  14.5 0.0 copy-start.4
  14.5 0.6 shard_map.56
  15.1 2.8 %all-to-all-done = bf16[16,16,128]{2,1,0:T(8,128)(2,1)S(1)} async-done(((bf16[16,16,128]{2,1,0:T(8,128)(2,1)}), bf16[16,16,128]{2,1,0:T(8,128)(2,1)S(1)}, u32[]{:S(2)}, u32[]{:S(2)}) %all-to-all-start) | async-done | bytes 65568 | tf_op jit(solution)/shard_map/all_to_all | solution.py:364
  17.8 0.8 %shard_map.57 = bf16[512,128]{1,0:T(8,128)(2,1)} custom-call(bf16[64,256]{1,0:T(8,128)(2,1)S(1)} %get-tuple-element.25.choice_ref, bf16[256,128]{1,0:T(8,128)(2,1)S(1)} %bitcast.13), custom_call_target="tpu_custom_call" | custom-call | bytes 229376 | tf_op jit(solution)/shard_map/pallas_call | solution.py:321
  18.6 10.9 %all-to-all-start.1 = ((bf16[8,64,128]{2,1,0:T(8,128)(2,1)}), bf16[8,64,128]{2,1,0:T(8,128)(2,1)S(1)}, u32[]{:S(2)}, u32[]{:S(2)}) async-start(bf16[8,64,128]{2,1,0:T(8,128)(2,1)} %bitcast.2), calls=%async_computation.1 | async-start | bytes 262144 | tf_op jit(solution)/shard_map/all_to_all | solution.py:376
  29.5 2.9 %collective-permute-start = (bf16[768,256]{1,0:T(8,128)(2,1)S(1)}, bf16[768,256]{1,0:T(8,128)(2,1)S(1)}, u32[]{:S(2)}, u32[]{:S(2)}) collective-permute-start(bf16[768,256]{1,0:T(8,128)(2,1)S(1)} %get-tuple-element.27), channel_id=1, source_target_pairs={{0,4},{4,8},{8,12},{12,16},{16,20},{20,24},{24,28},{28,32},{32,36}... | collective-permute-start | bytes 1179656 | tf_op jit(solution)/shard_map/ppermute | solution.py:375
  32.4 8.6 %collective-permute-done.halo_ref = bf16[768,256]{1,0:T(8,128)(2,1)S(1)} collective-permute-done((bf16[768,256]{1,0:T(8,128)(2,1)S(1)}, bf16[768,256]{1,0:T(8,128)(2,1)S(1)}, u32[]{:S(2)}, u32[]{:S(2)}) %collective-permute-start) | collective-permute-done | bytes 393248 | tf_op jit(solution)/shard_map/ppermute | solution.py:375
  41.0 2.0 %all-to-all-done.1 = bf16[8,64,128]{2,1,0:T(8,128)(2,1)S(1)} async-done(((bf16[8,64,128]{2,1,0:T(8,128)(2,1)}), bf16[8,64,128]{2,1,0:T(8,128)(2,1)S(1)}, u32[]{:S(2)}, u32[]{:S(2)}) %all-to-all-start.1) | async-done | bytes 131104 | tf_op jit(solution)/shard_map/all_to_all | solution.py:376
  42.9 0.7 shard_map.59
  43.7 7.1 %all-to-all-start.2 = ((bf16[16,64,128]{2,1,0:T(8,128)(2,1)}), bf16[16,64,128]{2,1,0:T(8,128)(2,1)S(1)}, u32[]{:S(2)}, u32[]{:S(2)}) async-start(bf16[16,64,128]{2,1,0:T(8,128)(2,1)} %bitcast.4), calls=%async_computation.2 | async-start | bytes 524288 | tf_op jit(solution)/shard_map/all_to_all | solution.py:386
  50.8 0.0 copy-done.6
  50.8 0.0 copy-done.3
  50.8 0.0 copy-done.1
  50.8 0.0 copy-done.7
  50.8 0.0 copy-done.4
  50.8 3.7 %shard_map.58 = (f32[384,1024]{1,0:T(8,128)S(1)}, f32[48,128]{1,0:T(8,128)S(1)}, s32[8,256]{1,0:T(8,128)S(1)}) custom-call(s32[2,4]{1,0:T(2,128)S(1)} %copy-done.6, s32[2,3]{1,0:T(2,128)S(1)} %copy-done.7, bf16[384,1024]{1,0:T(8,128)(2,1)S(1)} %copy-done.4, bf16[384,256]{1,0:T(8,128)(2,1)S(1)} %copy-done.1, bf16[384,256]{1,0:T(8,128)(2,1)S(1)} %copy-done.3, ...), custom_call_target="tpu_custom_call" | custom-call | flops 603979776 | bytes 3178496 | tf_op jit(solution)/shard_map/pallas_call | solution.py:321
  54.5 3.5 %all-to-all-done.2 = bf16[16,64,128]{2,1,0:T(8,128)(2,1)S(1)} async-done(((bf16[16,64,128]{2,1,0:T(8,128)(2,1)}), bf16[16,64,128]{2,1,0:T(8,128)(2,1)S(1)}, u32[]{:S(2)}, u32[]{:S(2)}) %all-to-all-start.2) | async-done | bytes 262176 | tf_op jit(solution)/shard_map/all_to_all | solution.py:386
  58.0 2.4 %shard_map.60 = bf16[384,1024]{1,0:T(8,128)(2,1)S(1)} custom-call(s32[8,256]{1,0:T(8,128)S(1)} %get-tuple-element.29.place_ref, bf16[384,1024]{1,0:T(8,128)(2,1)S(1)} %copy-done.4, bf16[1024,128]{1,0:T(8,128)(2,1)S(1)} %bitcast.11, f32[384,1024]{1,0:T(8,128)S(1)} %get-tuple-element.31.mixed_ref, f32[48,128]{1,0:T(8,128)S(1)} %get-tuple-element.32.level_ref), custom_call_target="tpu_custom_call" | custom-call | flops 402653184 | bytes 3440640 | tf_op jit(solution)/shard_map/pallas_call | solution.py:321
  60.4 14.7 %all_to_all.54 = bf16[4,96,1024]{2,1,0:T(8,128)(2,1)S(1)} all-to-all(bf16[4,96,1024]{2,1,0:T(8,128)(2,1)S(1)} %bitcast.10), channel_id=1, replica_groups=mesh['ctx'=128,'kvh'=4] {'kvh'}, dimensions={0} | all-to-all | bytes 1572864 | tf_op jit(solution)/shard_map/all_to_all | solution.py:413
  75.1 0.9 %copy.7 = bf16[4,12,8,1024]{3,2,0,1:T(8,128)(2,1)} copy(bf16[4,12,8,1024]{3,2,1,0:T(8,128)(2,1)S(1)} %bitcast.14) | data formatting | bytes 1572864 | tf_op jit(solution)/shard_map/all_to_all | solution.py:413
Async XLA Ops:
  0.0 50.8 %copy-start.6 = (s32[2,4]{1,0:T(2,128)S(1)}, s32[2,4]{1,0:T(2,128)}, u32[]{:S(2)}) copy-start(s32[2,4]{1,0:T(2,128)} %vert_ref.2) | copy-start | bytes 100
  0.0 50.8 %copy-start.3 = (bf16[384,256]{1,0:T(8,128)(2,1)S(1)}, bf16[384,256]{1,0:T(8,128)(2,1)}, u32[]{:S(2)}) copy-start(bf16[384,256]{1,0:T(8,128)(2,1)} %v_ref.2) | copy-start | bytes 589828
  0.0 50.8 %copy-start.1 = (bf16[384,256]{1,0:T(8,128)(2,1)S(1)}, bf16[384,256]{1,0:T(8,128)(2,1)}, u32[]{:S(2)}) copy-start(bf16[384,256]{1,0:T(8,128)(2,1)} %k_ref.2) | copy-start | bytes 589828
  0.0 50.8 %copy-start.7 = (s32[2,3]{1,0:T(2,128)S(1)}, s32[2,3]{1,0:T(2,128)}, u32[]{:S(2)}) copy-start(s32[2,3]{1,0:T(2,128)} %off_ref.1) | copy-start | bytes 76
  1.8 16.1 %all-to-all-start = ((bf16[16,16,128]{2,1,0:T(8,128)(2,1)}), bf16[16,16,128]{2,1,0:T(8,128)(2,1)S(1)}, u32[]{:S(2)}, u32[]{:S(2)}) async-start(bf16[16,16,128]{2,1,0:T(8,128)(2,1)} %bitcast.15), calls=%async_computation | async-start | bytes 131072 | tf_op jit(solution)/shard_map/all_to_all | solution.py:364
  11.9 0.9 %copy-start = (bf16[384,256]{1,0:T(8,128)(2,1)S(1)}, bf16[384,256]{1,0:T(8,128)(2,1)}, u32[]{:S(2)}) copy-start(bf16[384,256]{1,0:T(8,128)(2,1)} %k_ref.2) | copy-start | bytes 589828
  12.9 0.9 %copy-start.2 = (bf16[384,256]{1,0:T(8,128)(2,1)S(1)}, bf16[384,256]{1,0:T(8,128)(2,1)}, u32[]{:S(2)}) copy-start(bf16[384,256]{1,0:T(8,128)(2,1)} %v_ref.2) | copy-start | bytes 589828
  13.8 0.7 copy-start.5
  14.5 36.4 %copy-start.4 = (bf16[384,1024]{1,0:T(8,128)(2,1)S(1)}, bf16[384,1024]{1,0:T(8,128)(2,1)}, u32[]{:S(2)}) copy-start(bf16[384,1024]{1,0:T(8,128)(2,1)} %q_ref.3) | copy-start | bytes 2359300
  18.6 24.3 %all-to-all-start.1 = ((bf16[8,64,128]{2,1,0:T(8,128)(2,1)}), bf16[8,64,128]{2,1,0:T(8,128)(2,1)S(1)}, u32[]{:S(2)}, u32[]{:S(2)}) async-start(bf16[8,64,128]{2,1,0:T(8,128)(2,1)} %bitcast.2), calls=%async_computation.1 | async-start | bytes 262144 | tf_op jit(solution)/shard_map/all_to_all | solution.py:376
  29.5 11.5 %collective-permute-start = (bf16[768,256]{1,0:T(8,128)(2,1)S(1)}, bf16[768,256]{1,0:T(8,128)(2,1)S(1)}, u32[]{:S(2)}, u32[]{:S(2)}) collective-permute-start(bf16[768,256]{1,0:T(8,128)(2,1)S(1)} %get-tuple-element.27), channel_id=1, source_target_pairs={{0,4},{4,8},{8,12},{12,16},{16,20},{20,24},{24,28},{28,32},{32,36}... | collective-permute-start | bytes 1179656 | tf_op jit(solution)/shard_map/ppermute | solution.py:375
  43.7 14.4 %all-to-all-start.2 = ((bf16[16,64,128]{2,1,0:T(8,128)(2,1)}), bf16[16,64,128]{2,1,0:T(8,128)(2,1)S(1)}, u32[]{:S(2)}, u32[]{:S(2)}) async-start(bf16[16,64,128]{2,1,0:T(8,128)(2,1)} %bitcast.4), calls=%async_computation.2 | async-start | bytes 524288 | tf_op jit(solution)/shard_map/all_to_all | solution.py:386

commit v4 on v3

--- a/solution.py
+++ b/solution.py
@@ -298,8 +298,21 @@
             unstack(out_ref, *spot, mixed / (totals[head] + fade))
 
 
+def side_kernel(got_ref, out_hbm, sems, *, parts):
+    rows, width = out_hbm.shape[0], got_ref.shape[1]
+    copies = [
+        pltpu.make_async_copy(
+            got_ref.at[pl.ds(i * rows, rows)], out_hbm.at[:, pl.ds(i * width, width)], sems.at[i]
+        )
+        for i in range(parts)
+    ]
+    for copy in copies:
+        copy.start()
+    for copy in copies:
+        copy.wait()
+
+
 SMEM = pl.BlockSpec(memory_space=pltpu.SMEM)
-VMEM = pl.BlockSpec(memory_space=pltpu.VMEM)
 
 
 VMEM_PACK = 60 * 1024 * 1024
@@ -314,15 +327,17 @@
     flops=0,
     transcendentals=0,
     space=pltpu.VMEM,
+    into=pltpu.VMEM,
     vmem=16 * 1024 * 1024,
 ):
     shapes = out_shape if isinstance(out_shape, tuple) else (out_shape,)
+    place = pl.BlockSpec(memory_space=into)
     moved = sum(a.size * a.dtype.itemsize for a in arrays + shapes)
     return pl.pallas_call(
         kernel,
         out_shape=out_shape,
         in_specs=[SMEM] * len(scalars) + [pl.BlockSpec(memory_space=space)] * len(arrays),
-        out_specs=tuple(VMEM for _ in shapes) if isinstance(out_shape, tuple) else VMEM,
+        out_specs=(place,) * len(shapes) if isinstance(out_shape, tuple) else place,
         scratch_shapes=list(scratch),
         compiler_params=pltpu.CompilerParams(vmem_limit_bytes=vmem),
         cost_estimate=pl.CostEstimate(
@@ -410,7 +425,16 @@
         flops=4 * vert_pairs * width,
         transcendentals=vert_pairs,
     )
-    return lax.all_to_all(joined, "kvh", split_axis=0, concat_axis=1, tiled=True)
+    parts = lax.axis_size("kvh")
+    got = lax.all_to_all(joined, "kvh", split_axis=0, concat_axis=0, tiled=True)
+    return call(
+        functools.partial(side_kernel, parts=parts),
+        brief((tok_rows // parts, parts * queries.shape[1]), queries.dtype),
+        (),
+        (got,),
+        scratch=(pltpu.SemaphoreType.DMA((parts,)),),
+        into=pltpu.HBM,
+    )
 
 
 def solution(mesh):

time: 76.8 us -> 76.8 us (level)
  Pallas kernels: 9.86 us -> 10.8 us
  local copies, waits for them, and re-layouts: 3.48 us -> 2.54 us
    all_to_all x1 -> x0, local copies, waits for them, and re-layouts: 0.93 us -> none  [per_device(): lax.all_to_all(joined, 'kvh', split_axis=0, concat_axis=1, tiled=True)]
    pallas_call x6 -> x7, Pallas kernels: 9.86 us -> 10.8 us  [call(): pl.pallas_call(kernel, out_shape=out_shape, in_specs=[SMEM] * len(scalars...]
where the time goes in v4:
time: 76.8 us; the launch traced here: 76 us
  starting transfers between devices  31 us (40%)
  waiting for transfers between devices  16.8 us (22%)
  blocking collectives  14.7 us (19%)
  Pallas kernels  10.8 us (14%)
  local copies, waits for them, and re-layouts  2.54 us (3%)
    all_to_all x2, starting transfers between devices, per_device(): lax.all_to_all(sent, 'ctx', split_axis=0, concat_axis=0, tiled=True, axis...  18 us
    all_to_all x1, blocking collectives, per_device(): got = lax.all_to_all(joined, 'kvh', split_axis=0, concat_axis=0, tiled=True)  14.7 us
    pallas_call x7, Pallas kernels, call(): pl.pallas_call(kernel, out_shape=out_shape, in_specs=[SMEM] * len(scalars...  10.8 us
    all_to_all x1, starting transfers between devices, per_device(): lax.all_to_all(chunk, 'ctx', split_axis=0, concat_axis=0, tiled=True, axi...  10.2 us
    ppermute x1, waiting for transfers between devices, per_device(): halo = lax.ppermute(both, 'ctx', [(i, i + 1) for i in range(devices - 1)])  8.61 us
    all_to_all x2, waiting for transfers between devices, per_device(): lax.all_to_all(sent, 'ctx', split_axis=0, concat_axis=0, tiled=True, axis...  5.47 us
    ppermute x1, starting transfers between devices, per_device(): halo = lax.ppermute(both, 'ctx', [(i, i + 1) for i in range(devices - 1)])  2.87 us
    all_to_all x1, waiting for transfers between devices, per_device(): lax.all_to_all(chunk, 'ctx', split_axis=0, concat_axis=0, tiled=True, axi...  2.75 us
  transfers between devices with their start and end apart: 4, of which 4 were waited for; matrix products, arithmetic and copies ran while one was open for 0% of the time, Pallas kernels for 6%

profile of v4, /device:TPU:1, one launch (start us, length us, event | category | flops | bytes accessed | tf_op | source)
XLA Modules:
  0.0 76.0 jit_solution(7933304671097627457)
XLA Ops:
  0.0 0.0 copy-start.6
  0.0 0.0 copy-start.3
  0.0 0.0 copy-start.1
  0.0 0.0 copy-start.7
  0.0 1.7 %shard_map.55 = bf16[256,128]{1,0:T(8,128)(2,1)} custom-call(s32[2,4]{1,0:T(2,128)} %vert_ref.2, bf16[384,256]{1,0:T(8,128)(2,1)} %k_ref.2, bf16[384,256]{1,0:T(8,128)(2,1)} %v_ref.2), custom_call_target="tpu_custom_call" | custom-call | bytes 458784 | tf_op jit(solution)/shard_map/pallas_call | solution.py:336
  1.8 10.2 %all-to-all-start = ((bf16[16,16,128]{2,1,0:T(8,128)(2,1)}), bf16[16,16,128]{2,1,0:T(8,128)(2,1)S(1)}, u32[]{:S(2)}, u32[]{:S(2)}) async-start(bf16[16,16,128]{2,1,0:T(8,128)(2,1)} %bitcast.13), calls=%async_computation | async-start | bytes 131072 | tf_op jit(solution)/shard_map/all_to_all | solution.py:379
  11.9 0.0 copy-start
  11.9 0.9 %copy-done = bf16[384,256]{1,0:T(8,128)(2,1)S(1)} copy-done((bf16[384,256]{1,0:T(8,128)(2,1)S(1)}, bf16[384,256]{1,0:T(8,128)(2,1)}, u32[]{:S(2)}) %copy-start) | copy-done | bytes 196632
  12.9 0.0 copy-start.2
  12.9 0.9 %copy-done.2 = bf16[384,256]{1,0:T(8,128)(2,1)S(1)} copy-done((bf16[384,256]{1,0:T(8,128)(2,1)S(1)}, bf16[384,256]{1,0:T(8,128)(2,1)}, u32[]{:S(2)}) %copy-start.2) | copy-done | bytes 196632
  13.8 0.0 copy-start.5
  13.8 0.7 copy-done.5
  14.5 0.0 copy-start.4
  14.5 0.6 shard_map.56
  15.1 2.8 %all-to-all-done = bf16[16,16,128]{2,1,0:T(8,128)(2,1)S(1)} async-done(((bf16[16,16,128]{2,1,0:T(8,128)(2,1)}), bf16[16,16,128]{2,1,0:T(8,128)(2,1)S(1)}, u32[]{:S(2)}, u32[]{:S(2)}) %all-to-all-start) | async-done | bytes 65568 | tf_op jit(solution)/shard_map/all_to_all | solution.py:379
  17.8 0.8 %shard_map.57 = bf16[512,128]{1,0:T(8,128)(2,1)} custom-call(bf16[64,256]{1,0:T(8,128)(2,1)S(1)} %get-tuple-element.25.choice_ref, bf16[256,128]{1,0:T(8,128)(2,1)S(1)} %bitcast.12), custom_call_target="tpu_custom_call" | custom-call | bytes 229376 | tf_op jit(solution)/shard_map/pallas_call | solution.py:336
  18.6 10.9 %all-to-all-start.1 = ((bf16[8,64,128]{2,1,0:T(8,128)(2,1)}), bf16[8,64,128]{2,1,0:T(8,128)(2,1)S(1)}, u32[]{:S(2)}, u32[]{:S(2)}) async-start(bf16[8,64,128]{2,1,0:T(8,128)(2,1)} %bitcast.2), calls=%async_computation.1 | async-start | bytes 262144 | tf_op jit(solution)/shard_map/all_to_all | solution.py:391
  29.5 2.9 %collective-permute-start = (bf16[768,256]{1,0:T(8,128)(2,1)S(1)}, bf16[768,256]{1,0:T(8,128)(2,1)S(1)}, u32[]{:S(2)}, u32[]{:S(2)}) collective-permute-start(bf16[768,256]{1,0:T(8,128)(2,1)S(1)} %get-tuple-element.27), channel_id=1, source_target_pairs={{0,4},{4,8},{8,12},{12,16},{16,20},{20,24},{24,28},{28,32},{32,36}... | collective-permute-start | bytes 1179656 | tf_op jit(solution)/shard_map/ppermute | solution.py:390
  32.4 8.6 %collective-permute-done.halo_ref = bf16[768,256]{1,0:T(8,128)(2,1)S(1)} collective-permute-done((bf16[768,256]{1,0:T(8,128)(2,1)S(1)}, bf16[768,256]{1,0:T(8,128)(2,1)S(1)}, u32[]{:S(2)}, u32[]{:S(2)}) %collective-permute-start) | collective-permute-done | bytes 393248 | tf_op jit(solution)/shard_map/ppermute | solution.py:390
  41.0 2.0 %all-to-all-done.1 = bf16[8,64,128]{2,1,0:T(8,128)(2,1)S(1)} async-done(((bf16[8,64,128]{2,1,0:T(8,128)(2,1)}), bf16[8,64,128]{2,1,0:T(8,128)(2,1)S(1)}, u32[]{:S(2)}, u32[]{:S(2)}) %all-to-all-start.1) | async-done | bytes 131104 | tf_op jit(solution)/shard_map/all_to_all | solution.py:391
  42.9 0.7 shard_map.59
  43.7 7.1 %all-to-all-start.2 = ((bf16[16,64,128]{2,1,0:T(8,128)(2,1)}), bf16[16,64,128]{2,1,0:T(8,128)(2,1)S(1)}, u32[]{:S(2)}, u32[]{:S(2)}) async-start(bf16[16,64,128]{2,1,0:T(8,128)(2,1)} %bitcast.4), calls=%async_computation.2 | async-start | bytes 524288 | tf_op jit(solution)/shard_map/all_to_all | solution.py:401
  50.8 0.0 copy-done.6
  50.8 0.0 copy-done.3
  50.8 0.0 copy-done.1
  50.8 0.0 copy-done.7
  50.8 0.0 copy-done.4
  50.8 3.7 %shard_map.58 = (f32[384,1024]{1,0:T(8,128)S(1)}, f32[48,128]{1,0:T(8,128)S(1)}, s32[8,256]{1,0:T(8,128)S(1)}) custom-call(s32[2,4]{1,0:T(2,128)S(1)} %copy-done.6, s32[2,3]{1,0:T(2,128)S(1)} %copy-done.7, bf16[384,1024]{1,0:T(8,128)(2,1)S(1)} %copy-done.4, bf16[384,256]{1,0:T(8,128)(2,1)S(1)} %copy-done.1, bf16[384,256]{1,0:T(8,128)(2,1)S(1)} %copy-done.3, ...), custom_call_target="tpu_custom_call" | custom-call | flops 603979776 | bytes 3178496 | tf_op jit(solution)/shard_map/pallas_call | solution.py:336
  54.5 3.5 %all-to-all-done.2 = bf16[16,64,128]{2,1,0:T(8,128)(2,1)S(1)} async-done(((bf16[16,64,128]{2,1,0:T(8,128)(2,1)}), bf16[16,64,128]{2,1,0:T(8,128)(2,1)S(1)}, u32[]{:S(2)}, u32[]{:S(2)}) %all-to-all-start.2) | async-done | bytes 262176 | tf_op jit(solution)/shard_map/all_to_all | solution.py:401
  58.0 2.4 %shard_map.60 = bf16[384,1024]{1,0:T(8,128)(2,1)S(1)} custom-call(s32[8,256]{1,0:T(8,128)S(1)} %get-tuple-element.29.place_ref, bf16[384,1024]{1,0:T(8,128)(2,1)S(1)} %copy-done.4, bf16[1024,128]{1,0:T(8,128)(2,1)S(1)} %bitcast.10, f32[384,1024]{1,0:T(8,128)S(1)} %get-tuple-element.31.mixed_ref, f32[48,128]{1,0:T(8,128)S(1)} %get-tuple-element.32.level_ref), custom_call_target="tpu_custom_call" | custom-call | flops 402653184 | bytes 3440640 | tf_op jit(solution)/shard_map/pallas_call | solution.py:336
  60.4 14.7 %all_to_all.46 = bf16[4,96,1024]{2,1,0:T(8,128)(2,1)S(1)} all-to-all(bf16[4,96,1024]{2,1,0:T(8,128)(2,1)S(1)} %bitcast.9), channel_id=1, replica_groups=mesh['ctx'=128,'kvh'=4] {'kvh'}, dimensions={0} | all-to-all | bytes 1572864 | tf_op jit(solution)/shard_map/all_to_all | solution.py:429
  75.1 0.9 %shard_map.61 = bf16[96,4096]{1,0:T(8,128)(2,1)} custom-call(bf16[384,1024]{1,0:T(8,128)(2,1)S(1)} %bitcast.8), custom_call_target="tpu_custom_call" | custom-call | bytes 1572864 | tf_op jit(solution)/shard_map/pallas_call | solution.py:336
Async XLA Ops:
  0.0 50.8 %copy-start.6 = (s32[2,4]{1,0:T(2,128)S(1)}, s32[2,4]{1,0:T(2,128)}, u32[]{:S(2)}) copy-start(s32[2,4]{1,0:T(2,128)} %vert_ref.2) | copy-start | bytes 100
  0.0 50.8 %copy-start.3 = (bf16[384,256]{1,0:T(8,128)(2,1)S(1)}, bf16[384,256]{1,0:T(8,128)(2,1)}, u32[]{:S(2)}) copy-start(bf16[384,256]{1,0:T(8,128)(2,1)} %v_ref.2) | copy-start | bytes 589828
  0.0 50.8 %copy-start.1 = (bf16[384,256]{1,0:T(8,128)(2,1)S(1)}, bf16[384,256]{1,0:T(8,128)(2,1)}, u32[]{:S(2)}) copy-start(bf16[384,256]{1,0:T(8,128)(2,1)} %k_ref.2) | copy-start | bytes 589828
  0.0 50.8 %copy-start.7 = (s32[2,3]{1,0:T(2,128)S(1)}, s32[2,3]{1,0:T(2,128)}, u32[]{:S(2)}) copy-start(s32[2,3]{1,0:T(2,128)} %off_ref.1) | copy-start | bytes 76
  1.8 16.1 %all-to-all-start = ((bf16[16,16,128]{2,1,0:T(8,128)(2,1)}), bf16[16,16,128]{2,1,0:T(8,128)(2,1)S(1)}, u32[]{:S(2)}, u32[]{:S(2)}) async-start(bf16[16,16,128]{2,1,0:T(8,128)(2,1)} %bitcast.13), calls=%async_computation | async-start | bytes 131072 | tf_op jit(solution)/shard_map/all_to_all | solution.py:379
  11.9 0.9 %copy-start = (bf16[384,256]{1,0:T(8,128)(2,1)S(1)}, bf16[384,256]{1,0:T(8,128)(2,1)}, u32[]{:S(2)}) copy-start(bf16[384,256]{1,0:T(8,128)(2,1)} %k_ref.2) | copy-start | bytes 589828
  12.9 0.9 %copy-start.2 = (bf16[384,256]{1,0:T(8,128)(2,1)S(1)}, bf16[384,256]{1,0:T(8,128)(2,1)}, u32[]{:S(2)}) copy-start(bf16[384,256]{1,0:T(8,128)(2,1)} %v_ref.2) | copy-start | bytes 589828
  13.8 0.7 copy-start.5
  14.5 36.4 %copy-start.4 = (bf16[384,1024]{1,0:T(8,128)(2,1)S(1)}, bf16[384,1024]{1,0:T(8,128)(2,1)}, u32[]{:S(2)}) copy-start(bf16[384,1024]{1,0:T(8,128)(2,1)} %q_ref.3) | copy-start | bytes 2359300
  18.6 24.3 %all-to-all-start.1 = ((bf16[8,64,128]{2,1,0:T(8,128)(2,1)}), bf16[8,64,128]{2,1,0:T(8,128)(2,1)S(1)}, u32[]{:S(2)}, u32[]{:S(2)}) async-start(bf16[8,64,128]{2,1,0:T(8,128)(2,1)} %bitcast.2), calls=%async_computation.1 | async-start | bytes 262144 | tf_op jit(solution)/shard_map/all_to_all | solution.py:391
  29.5 11.5 %collective-permute-start = (bf16[768,256]{1,0:T(8,128)(2,1)S(1)}, bf16[768,256]{1,0:T(8,128)(2,1)S(1)}, u32[]{:S(2)}, u32[]{:S(2)}) collective-permute-start(bf16[768,256]{1,0:T(8,128)(2,1)S(1)} %get-tuple-element.27), channel_id=1, source_target_pairs={{0,4},{4,8},{8,12},{12,16},{16,20},{20,24},{24,28},{28,32},{32,36}... | collective-permute-start | bytes 1179656 | tf_op jit(solution)/shard_map/ppermute | solution.py:390
  43.7 14.4 %all-to-all-start.2 = ((bf16[16,64,128]{2,1,0:T(8,128)(2,1)}), bf16[16,64,128]{2,1,0:T(8,128)(2,1)S(1)}, u32[]{:S(2)}, u32[]{:S(2)}) async-start(bf16[16,64,128]{2,1,0:T(8,128)(2,1)} %bitcast.4), calls=%async_computation.2 | async-start | bytes 524288 | tf_op jit(solution)/shard_map/all_to_all | solution.py:401

commit v5 on v4

--- a/solution.py
+++ b/solution.py
@@ -117,21 +117,31 @@
             place_ref[at : at + 1, :] = jnp.full(col.shape, off_ref[head, b], jnp.int32)
 
 
-def near_pick_kernel(choice_ref, got_ref, out_ref):
+def spread_out(piece_ref, out_hbm, sems):
+    rows = piece_ref.shape[0]
+    copies = [
+        pltpu.make_async_copy(piece_ref, out_hbm.at[pl.ds(i * rows, rows)], sems.at[i])
+        for i in range(out_hbm.shape[0] // rows)
+    ]
+    for copy in copies:
+        copy.start()
+    for copy in copies:
+        copy.wait()
+
+
+def near_pick_kernel(choice_ref, got_ref, out_hbm, piece_ref, sems):
     pieces = jnp.dot(choice_ref[...], got_ref[...], preferred_element_type=jnp.float32)
-    pieces = pieces.astype(out_ref.dtype)
-    rows = pieces.shape[0]
-    for copy in range(N_FAR):
-        out_ref[copy * rows : (copy + 1) * rows, :] = pieces
-
-
-def far_pick_kernel(got_ref, out_ref):
+    piece_ref[...] = pieces.astype(piece_ref.dtype)
+    spread_out(piece_ref, out_hbm, sems)
+
+
+def far_pick_kernel(got_ref, out_hbm, piece_ref, sems):
     rows = got_ref.shape[0] // N_FAR
     total = got_ref[:rows, :]
     for source in range(1, N_FAR):
         total = total + got_ref[source * rows : (source + 1) * rows, :]
-    for copy in range(N_CLOSE):
-        out_ref[copy * rows : (copy + 1) * rows, :] = total
+    piece_ref[...] = total
+    spread_out(piece_ref, out_hbm, sems)
 
 
 def stacked(ref, low, rows, head, group, width):
@@ -385,6 +395,8 @@
         brief((N_FAR * strips, width), keys.dtype),
         (),
         (choice, got),
+        scratch=(pltpu.VMEM((strips, width), keys.dtype), pltpu.SemaphoreType.DMA((N_FAR,))),
+        into=pltpu.HBM,
     )
     devices = lax.axis_size("ctx")
     halo = lax.ppermute(both, "ctx", [(i, i + 1) for i in range(devices - 1)])
@@ -397,6 +409,8 @@
         brief((N_CLOSE * strips, width), keys.dtype),
         (),
         (got,),
+        scratch=(pltpu.VMEM((strips, width), keys.dtype), pltpu.SemaphoreType.DMA((N_CLOSE,))),
+        into=pltpu.HBM,
     )
     far = lax.all_to_all(
         sent, "ctx", split_axis=0, concat_axis=0, tiled=True, axis_index_groups=CLOSE_GROUPS

time: 76.8 us -> 77 us (level)
  no operation moved by 1% of the time
where the time goes in v5:
time: 77 us; the launch traced here: 76.2 us
  starting transfers between devices  31.1 us (40%)
  waiting for transfers between devices  16.8 us (22%)
  blocking collectives  14.7 us (19%)
  Pallas kernels  10.9 us (14%)
  local copies, waits for them, and re-layouts  2.54 us (3%)
    all_to_all x2, starting transfers between devices, per_device(): lax.all_to_all(sent, 'ctx', split_axis=0, concat_axis=0, tiled=True, axis...  18 us
    all_to_all x1, blocking collectives, per_device(): got = lax.all_to_all(joined, 'kvh', split_axis=0, concat_axis=0, tiled=True)  14.7 us
    pallas_call x7, Pallas kernels, call(): pl.pallas_call(kernel, out_shape=out_shape, in_specs=[SMEM] * len(scalars...  10.9 us
    all_to_all x1, starting transfers between devices, per_device(): lax.all_to_all(chunk, 'ctx', split_axis=0, concat_axis=0, tiled=True, axi...  10.2 us
    ppermute x1, waiting for transfers between devices, per_device(): halo = lax.ppermute(both, 'ctx', [(i, i + 1) for i in range(devices - 1)])  8.61 us
    all_to_all x2, waiting for transfers between devices, per_device(): lax.all_to_all(sent, 'ctx', split_axis=0, concat_axis=0, tiled=True, axis...  5.44 us
    ppermute x1, starting transfers between devices, per_device(): halo = lax.ppermute(both, 'ctx', [(i, i + 1) for i in range(devices - 1)])  2.87 us
    all_to_all x1, waiting for transfers between devices, per_device(): lax.all_to_all(chunk, 'ctx', split_axis=0, concat_axis=0, tiled=True, axi...  2.75 us
  transfers between devices with their start and end apart: 4, of which 4 were waited for; matrix products, arithmetic and copies ran while one was open for 0% of the time, Pallas kernels for 6%

profile of v5, /device:TPU:1, one launch (start us, length us, event | category | flops | bytes accessed | tf_op | source)
XLA Modules:
  0.0 76.2 jit_solution(15282426379423089305)
XLA Ops:
  0.0 0.0 copy-start.6
  0.0 0.0 copy-start.3
  0.0 0.0 copy-start.1
  0.0 0.0 copy-start.7
  0.0 1.7 %shard_map.55 = bf16[256,128]{1,0:T(8,128)(2,1)} custom-call(s32[2,4]{1,0:T(2,128)} %vert_ref.2, bf16[384,256]{1,0:T(8,128)(2,1)} %k_ref.2, bf16[384,256]{1,0:T(8,128)(2,1)} %v_ref.2), custom_call_target="tpu_custom_call" | custom-call | bytes 458784 | tf_op jit(solution)/shard_map/pallas_call | solution.py:346
  1.8 10.2 %all-to-all-start = ((bf16[16,16,128]{2,1,0:T(8,128)(2,1)}), bf16[16,16,128]{2,1,0:T(8,128)(2,1)S(1)}, u32[]{:S(2)}, u32[]{:S(2)}) async-start(bf16[16,16,128]{2,1,0:T(8,128)(2,1)} %bitcast.13), calls=%async_computation | async-start | bytes 131072 | tf_op jit(solution)/shard_map/all_to_all | solution.py:389
  11.9 0.0 copy-start
  11.9 0.9 %copy-done = bf16[384,256]{1,0:T(8,128)(2,1)S(1)} copy-done((bf16[384,256]{1,0:T(8,128)(2,1)S(1)}, bf16[384,256]{1,0:T(8,128)(2,1)}, u32[]{:S(2)}) %copy-start) | copy-done | bytes 196632
  12.9 0.0 copy-start.2
  12.9 0.9 %copy-done.2 = bf16[384,256]{1,0:T(8,128)(2,1)S(1)} copy-done((bf16[384,256]{1,0:T(8,128)(2,1)S(1)}, bf16[384,256]{1,0:T(8,128)(2,1)}, u32[]{:S(2)}) %copy-start.2) | copy-done | bytes 196632
  13.8 0.0 copy-start.5
  13.8 0.7 copy-done.5
  14.5 0.0 copy-start.4
  14.5 0.6 shard_map.56
  15.1 2.8 %all-to-all-done = bf16[16,16,128]{2,1,0:T(8,128)(2,1)S(1)} async-done(((bf16[16,16,128]{2,1,0:T(8,128)(2,1)}), bf16[16,16,128]{2,1,0:T(8,128)(2,1)S(1)}, u32[]{:S(2)}, u32[]{:S(2)}) %all-to-all-start) | async-done | bytes 65568 | tf_op jit(solution)/shard_map/all_to_all | solution.py:389
  17.8 0.9 %shard_map.57 = bf16[512,128]{1,0:T(8,128)(2,1)} custom-call(bf16[64,256]{1,0:T(8,128)(2,1)S(1)} %get-tuple-element.25.choice_ref, bf16[256,128]{1,0:T(8,128)(2,1)S(1)} %bitcast.12), custom_call_target="tpu_custom_call" | custom-call | bytes 229376 | tf_op jit(solution)/shard_map/pallas_call | solution.py:346
  18.7 10.9 %all-to-all-start.1 = ((bf16[8,64,128]{2,1,0:T(8,128)(2,1)}), bf16[8,64,128]{2,1,0:T(8,128)(2,1)S(1)}, u32[]{:S(2)}, u32[]{:S(2)}) async-start(bf16[8,64,128]{2,1,0:T(8,128)(2,1)} %bitcast.2), calls=%async_computation.1 | async-start | bytes 262144 | tf_op jit(solution)/shard_map/all_to_all | solution.py:403
  29.6 2.9 %collective-permute-start = (bf16[768,256]{1,0:T(8,128)(2,1)S(1)}, bf16[768,256]{1,0:T(8,128)(2,1)S(1)}, u32[]{:S(2)}, u32[]{:S(2)}) collective-permute-start(bf16[768,256]{1,0:T(8,128)(2,1)S(1)} %get-tuple-element.27), channel_id=1, source_target_pairs={{0,4},{4,8},{8,12},{12,16},{16,20},{20,24},{24,28},{28,32},{32,36}... | collective-permute-start | bytes 1179656 | tf_op jit(solution)/shard_map/ppermute | solution.py:402
  32.4 8.6 %collective-permute-done.halo_ref = bf16[768,256]{1,0:T(8,128)(2,1)S(1)} collective-permute-done((bf16[768,256]{1,0:T(8,128)(2,1)S(1)}, bf16[768,256]{1,0:T(8,128)(2,1)S(1)}, u32[]{:S(2)}, u32[]{:S(2)}) %collective-permute-start) | collective-permute-done | bytes 393248 | tf_op jit(solution)/shard_map/ppermute | solution.py:402
  41.0 2.0 %all-to-all-done.1 = bf16[8,64,128]{2,1,0:T(8,128)(2,1)S(1)} async-done(((bf16[8,64,128]{2,1,0:T(8,128)(2,1)}), bf16[8,64,128]{2,1,0:T(8,128)(2,1)S(1)}, u32[]{:S(2)}, u32[]{:S(2)}) %all-to-all-start.1) | async-done | bytes 131104 | tf_op jit(solution)/shard_map/all_to_all | solution.py:403
  43.0 0.8 %shard_map.59 = bf16[1024,128]{1,0:T(8,128)(2,1)} custom-call(bf16[512,128]{1,0:T(8,128)(2,1)S(1)} %bitcast.11), custom_call_target="tpu_custom_call" | custom-call | bytes 393216 | tf_op jit(solution)/shard_map/pallas_call | solution.py:346
  43.8 7.1 %all-to-all-start.2 = ((bf16[16,64,128]{2,1,0:T(8,128)(2,1)}), bf16[16,64,128]{2,1,0:T(8,128)(2,1)S(1)}, u32[]{:S(2)}, u32[]{:S(2)}) async-start(bf16[16,64,128]{2,1,0:T(8,128)(2,1)} %bitcast.4), calls=%async_computation.2 | async-start | bytes 524288 | tf_op jit(solution)/shard_map/all_to_all | solution.py:415
  51.0 0.0 copy-done.6
  51.0 0.0 copy-done.3
  51.0 0.0 copy-done.1
  51.0 0.0 copy-done.7
  51.0 0.0 copy-done.4
  51.0 3.7 %shard_map.58 = (f32[384,1024]{1,0:T(8,128)S(1)}, f32[48,128]{1,0:T(8,128)S(1)}, s32[8,256]{1,0:T(8,128)S(1)}) custom-call(s32[2,4]{1,0:T(2,128)S(1)} %copy-done.6, s32[2,3]{1,0:T(2,128)S(1)} %copy-done.7, bf16[384,1024]{1,0:T(8,128)(2,1)S(1)} %copy-done.4, bf16[384,256]{1,0:T(8,128)(2,1)S(1)} %copy-done.1, bf16[384,256]{1,0:T(8,128)(2,1)S(1)} %copy-done.3, ...), custom_call_target="tpu_custom_call" | custom-call | flops 603979776 | bytes 3178496 | tf_op jit(solution)/shard_map/pallas_call | solution.py:346
  54.7 3.5 %all-to-all-done.2 = bf16[16,64,128]{2,1,0:T(8,128)(2,1)S(1)} async-done(((bf16[16,64,128]{2,1,0:T(8,128)(2,1)}), bf16[16,64,128]{2,1,0:T(8,128)(2,1)S(1)}, u32[]{:S(2)}, u32[]{:S(2)}) %all-to-all-start.2) | async-done | bytes 262176 | tf_op jit(solution)/shard_map/all_to_all | solution.py:415
  58.2 2.3 %shard_map.60 = bf16[384,1024]{1,0:T(8,128)(2,1)S(1)} custom-call(s32[8,256]{1,0:T(8,128)S(1)} %get-tuple-element.29.place_ref, bf16[384,1024]{1,0:T(8,128)(2,1)S(1)} %copy-done.4, bf16[1024,128]{1,0:T(8,128)(2,1)S(1)} %bitcast.10, f32[384,1024]{1,0:T(8,128)S(1)} %get-tuple-element.31.mixed_ref, f32[48,128]{1,0:T(8,128)S(1)} %get-tuple-element.32.level_ref), custom_call_target="tpu_custom_call" | custom-call | flops 402653184 | bytes 3440640 | tf_op jit(solution)/shard_map/pallas_call | solution.py:346
  60.6 14.7 %all_to_all.46 = bf16[4,96,1024]{2,1,0:T(8,128)(2,1)S(1)} all-to-all(bf16[4,96,1024]{2,1,0:T(8,128)(2,1)S(1)} %bitcast.9), channel_id=1, replica_groups=mesh['ctx'=128,'kvh'=4] {'kvh'}, dimensions={0} | all-to-all | bytes 1572864 | tf_op jit(solution)/shard_map/all_to_all | solution.py:443
  75.3 0.9 %shard_map.61 = bf16[96,4096]{1,0:T(8,128)(2,1)} custom-call(bf16[384,1024]{1,0:T(8,128)(2,1)S(1)} %bitcast.8), custom_call_target="tpu_custom_call" | custom-call | bytes 1572864 | tf_op jit(solution)/shard_map/pallas_call | solution.py:346
Async XLA Ops:
  0.0 51.0 %copy-start.6 = (s32[2,4]{1,0:T(2,128)S(1)}, s32[2,4]{1,0:T(2,128)}, u32[]{:S(2)}) copy-start(s32[2,4]{1,0:T(2,128)} %vert_ref.2) | copy-start | bytes 100
  0.0 51.0 %copy-start.3 = (bf16[384,256]{1,0:T(8,128)(2,1)S(1)}, bf16[384,256]{1,0:T(8,128)(2,1)}, u32[]{:S(2)}) copy-start(bf16[384,256]{1,0:T(8,128)(2,1)} %v_ref.2) | copy-start | bytes 589828
  0.0 51.0 %copy-start.1 = (bf16[384,256]{1,0:T(8,128)(2,1)S(1)}, bf16[384,256]{1,0:T(8,128)(2,1)}, u32[]{:S(2)}) copy-start(bf16[384,256]{1,0:T(8,128)(2,1)} %k_ref.2) | copy-start | bytes 589828
  0.0 51.0 %copy-start.7 = (s32[2,3]{1,0:T(2,128)S(1)}, s32[2,3]{1,0:T(2,128)}, u32[]{:S(2)}) copy-start(s32[2,3]{1,0:T(2,128)} %off_ref.1) | copy-start | bytes 76
  1.8 16.1 %all-to-all-start = ((bf16[16,16,128]{2,1,0:T(8,128)(2,1)}), bf16[16,16,128]{2,1,0:T(8,128)(2,1)S(1)}, u32[]{:S(2)}, u32[]{:S(2)}) async-start(bf16[16,16,128]{2,1,0:T(8,128)(2,1)} %bitcast.13), calls=%async_computation | async-start | bytes 131072 | tf_op jit(solution)/shard_map/all_to_all | solution.py:389
  11.9 0.9 %copy-start = (bf16[384,256]{1,0:T(8,128)(2,1)S(1)}, bf16[384,256]{1,0:T(8,128)(2,1)}, u32[]{:S(2)}) copy-start(bf16[384,256]{1,0:T(8,128)(2,1)} %k_ref.2) | copy-start | bytes 589828
  12.9 0.9 %copy-start.2 = (bf16[384,256]{1,0:T(8,128)(2,1)S(1)}, bf16[384,256]{1,0:T(8,128)(2,1)}, u32[]{:S(2)}) copy-start(bf16[384,256]{1,0:T(8,128)(2,1)} %v_ref.2) | copy-start | bytes 589828
  13.8 0.7 copy-start.5
  14.5 36.6 %copy-start.4 = (bf16[384,1024]{1,0:T(8,128)(2,1)S(1)}, bf16[384,1024]{1,0:T(8,128)(2,1)}, u32[]{:S(2)}) copy-start(bf16[384,1024]{1,0:T(8,128)(2,1)} %q_ref.3) | copy-start | bytes 2359300
  18.7 24.3 %all-to-all-start.1 = ((bf16[8,64,128]{2,1,0:T(8,128)(2,1)}), bf16[8,64,128]{2,1,0:T(8,128)(2,1)S(1)}, u32[]{:S(2)}, u32[]{:S(2)}) async-start(bf16[8,64,128]{2,1,0:T(8,128)(2,1)} %bitcast.2), calls=%async_computation.1 | async-start | bytes 262144 | tf_op jit(solution)/shard_map/all_to_all | solution.py:403
  29.6 11.5 %collective-permute-start = (bf16[768,256]{1,0:T(8,128)(2,1)S(1)}, bf16[768,256]{1,0:T(8,128)(2,1)S(1)}, u32[]{:S(2)}, u32[]{:S(2)}) collective-permute-start(bf16[768,256]{1,0:T(8,128)(2,1)S(1)} %get-tuple-element.27), channel_id=1, source_target_pairs={{0,4},{4,8},{8,12},{12,16},{16,20},{20,24},{24,28},{28,32},{32,36}... | collective-permute-start | bytes 1179656 | tf_op jit(solution)/shard_map/ppermute | solution.py:402
  43.8 14.4 %all-to-all-start.2 = ((bf16[16,64,128]{2,1,0:T(8,128)(2,1)}), bf16[16,64,128]{2,1,0:T(8,128)(2,1)S(1)}, u32[]{:S(2)}, u32[]{:S(2)}) async-start(bf16[16,64,128]{2,1,0:T(8,128)(2,1)} %bitcast.4), calls=%async_computation.2 | async-start | bytes 524288 | tf_op jit(solution)/shard_map/all_to_all | solution.py:415

commit v6 on v4

--- a/solution.py
+++ b/solution.py
@@ -11,7 +11,7 @@
 TILE = 16
 LANES = 128
 SLASH_ROWS = 48
-VERT_ROWS = 2 * SLASH_ROWS
+VERT_ROWS = 4 * SLASH_ROWS
 NEG = -1e30
 LOG2E = 1.4426950408889634
 

time: 76.8 us -> 76.7 us (level)
  no operation moved by 1% of the time
where the time goes in v6:
time: 76.7 us; the launch traced here: 75.9 us
  starting transfers between devices  31 us (40%)
  waiting for transfers between devices  16.8 us (22%)
  blocking collectives  14.7 us (19%)
  Pallas kernels  10.7 us (14%)
  local copies, waits for them, and re-layouts  2.54 us (3%)
    all_to_all x2, starting transfers between devices, per_device(): lax.all_to_all(sent, 'ctx', split_axis=0, concat_axis=0, tiled=True, axis...  18 us
    all_to_all x1, blocking collectives, per_device(): got = lax.all_to_all(joined, 'kvh', split_axis=0, concat_axis=0, tiled=True)  14.7 us
    pallas_call x7, Pallas kernels, call(): pl.pallas_call(kernel, out_shape=out_shape, in_specs=[SMEM] * len(scalars...  10.7 us
    all_to_all x1, starting transfers between devices, per_device(): lax.all_to_all(chunk, 'ctx', split_axis=0, concat_axis=0, tiled=True, axi...  10.2 us
    ppermute x1, waiting for transfers between devices, per_device(): halo = lax.ppermute(both, 'ctx', [(i, i + 1) for i in range(devices - 1)])  8.61 us
    all_to_all x2, waiting for transfers between devices, per_device(): lax.all_to_all(sent, 'ctx', split_axis=0, concat_axis=0, tiled=True, axis...  5.44 us
    ppermute x1, starting transfers between devices, per_device(): halo = lax.ppermute(both, 'ctx', [(i, i + 1) for i in range(devices - 1)])  2.87 us
    all_to_all x1, waiting for transfers between devices, per_device(): lax.all_to_all(chunk, 'ctx', split_axis=0, concat_axis=0, tiled=True, axi...  2.75 us
  transfers between devices with their start and end apart: 4, of which 4 were waited for; matrix products, arithmetic and copies ran while one was open for 0% of the time, Pallas kernels for 6%

profile of v6, /device:TPU:1, one launch (start us, length us, event | category | flops | bytes accessed | tf_op | source)
XLA Modules:
  0.0 75.9 jit_solution(2903881143250290726)
XLA Ops:
  0.0 0.0 copy-start.6
  0.0 0.0 copy-start.3
  0.0 0.0 copy-start.1
  0.0 0.0 copy-start.7
  0.0 1.7 %shard_map.55 = bf16[256,128]{1,0:T(8,128)(2,1)} custom-call(s32[2,4]{1,0:T(2,128)} %vert_ref.2, bf16[384,256]{1,0:T(8,128)(2,1)} %k_ref.2, bf16[384,256]{1,0:T(8,128)(2,1)} %v_ref.2), custom_call_target="tpu_custom_call" | custom-call | bytes 458784 | tf_op jit(solution)/shard_map/pallas_call | solution.py:336
  1.8 10.2 %all-to-all-start = ((bf16[16,16,128]{2,1,0:T(8,128)(2,1)}), bf16[16,16,128]{2,1,0:T(8,128)(2,1)S(1)}, u32[]{:S(2)}, u32[]{:S(2)}) async-start(bf16[16,16,128]{2,1,0:T(8,128)(2,1)} %bitcast.13), calls=%async_computation | async-start | bytes 131072 | tf_op jit(solution)/shard_map/all_to_all | solution.py:379
  11.9 0.0 copy-start
  11.9 0.9 %copy-done = bf16[384,256]{1,0:T(8,128)(2,1)S(1)} copy-done((bf16[384,256]{1,0:T(8,128)(2,1)S(1)}, bf16[384,256]{1,0:T(8,128)(2,1)}, u32[]{:S(2)}) %copy-start) | copy-done | bytes 196632
  12.9 0.0 copy-start.2
  12.9 0.9 %copy-done.2 = bf16[384,256]{1,0:T(8,128)(2,1)S(1)} copy-done((bf16[384,256]{1,0:T(8,128)(2,1)S(1)}, bf16[384,256]{1,0:T(8,128)(2,1)}, u32[]{:S(2)}) %copy-start.2) | copy-done | bytes 196632
  13.8 0.0 copy-start.5
  13.8 0.7 copy-done.5
  14.5 0.0 copy-start.4
  14.5 0.6 shard_map.56
  15.1 2.8 %all-to-all-done = bf16[16,16,128]{2,1,0:T(8,128)(2,1)S(1)} async-done(((bf16[16,16,128]{2,1,0:T(8,128)(2,1)}), bf16[16,16,128]{2,1,0:T(8,128)(2,1)S(1)}, u32[]{:S(2)}, u32[]{:S(2)}) %all-to-all-start) | async-done | bytes 65568 | tf_op jit(solution)/shard_map/all_to_all | solution.py:379
  17.8 0.8 %shard_map.57 = bf16[512,128]{1,0:T(8,128)(2,1)} custom-call(bf16[64,256]{1,0:T(8,128)(2,1)S(1)} %get-tuple-element.25.choice_ref, bf16[256,128]{1,0:T(8,128)(2,1)S(1)} %bitcast.12), custom_call_target="tpu_custom_call" | custom-call | bytes 229376 | tf_op jit(solution)/shard_map/pallas_call | solution.py:336
  18.6 10.9 %all-to-all-start.1 = ((bf16[8,64,128]{2,1,0:T(8,128)(2,1)}), bf16[8,64,128]{2,1,0:T(8,128)(2,1)S(1)}, u32[]{:S(2)}, u32[]{:S(2)}) async-start(bf16[8,64,128]{2,1,0:T(8,128)(2,1)} %bitcast.2), calls=%async_computation.1 | async-start | bytes 262144 | tf_op jit(solution)/shard_map/all_to_all | solution.py:391
  29.5 2.9 %collective-permute-start = (bf16[768,256]{1,0:T(8,128)(2,1)S(1)}, bf16[768,256]{1,0:T(8,128)(2,1)S(1)}, u32[]{:S(2)}, u32[]{:S(2)}) collective-permute-start(bf16[768,256]{1,0:T(8,128)(2,1)S(1)} %get-tuple-element.27), channel_id=1, source_target_pairs={{0,4},{4,8},{8,12},{12,16},{16,20},{20,24},{24,28},{28,32},{32,36}... | collective-permute-start | bytes 1179656 | tf_op jit(solution)/shard_map/ppermute | solution.py:390
  32.4 8.6 %collective-permute-done.halo_ref = bf16[768,256]{1,0:T(8,128)(2,1)S(1)} collective-permute-done((bf16[768,256]{1,0:T(8,128)(2,1)S(1)}, bf16[768,256]{1,0:T(8,128)(2,1)S(1)}, u32[]{:S(2)}, u32[]{:S(2)}) %collective-permute-start) | collective-permute-done | bytes 393248 | tf_op jit(solution)/shard_map/ppermute | solution.py:390
  41.0 2.0 %all-to-all-done.1 = bf16[8,64,128]{2,1,0:T(8,128)(2,1)S(1)} async-done(((bf16[8,64,128]{2,1,0:T(8,128)(2,1)}), bf16[8,64,128]{2,1,0:T(8,128)(2,1)S(1)}, u32[]{:S(2)}, u32[]{:S(2)}) %all-to-all-start.1) | async-done | bytes 131104 | tf_op jit(solution)/shard_map/all_to_all | solution.py:391
  42.9 0.7 shard_map.59
  43.7 7.1 %all-to-all-start.2 = ((bf16[16,64,128]{2,1,0:T(8,128)(2,1)}), bf16[16,64,128]{2,1,0:T(8,128)(2,1)S(1)}, u32[]{:S(2)}, u32[]{:S(2)}) async-start(bf16[16,64,128]{2,1,0:T(8,128)(2,1)} %bitcast.4), calls=%async_computation.2 | async-start | bytes 524288 | tf_op jit(solution)/shard_map/all_to_all | solution.py:401
  50.8 0.0 copy-done.6
  50.8 0.0 copy-done.3
  50.8 0.0 copy-done.1
  50.8 0.0 copy-done.7
  50.8 0.0 copy-done.4
  50.8 3.7 %shard_map.58 = (f32[384,1024]{1,0:T(8,128)S(1)}, f32[48,128]{1,0:T(8,128)S(1)}, s32[8,256]{1,0:T(8,128)S(1)}) custom-call(s32[2,4]{1,0:T(2,128)S(1)} %copy-done.6, s32[2,3]{1,0:T(2,128)S(1)} %copy-done.7, bf16[384,1024]{1,0:T(8,128)(2,1)S(1)} %copy-done.4, bf16[384,256]{1,0:T(8,128)(2,1)S(1)} %copy-done.1, bf16[384,256]{1,0:T(8,128)(2,1)S(1)} %copy-done.3, ...), custom_call_target="tpu_custom_call" | custom-call | flops 603979776 | bytes 3178496 | tf_op jit(solution)/shard_map/pallas_call | solution.py:336
  54.5 3.5 %all-to-all-done.2 = bf16[16,64,128]{2,1,0:T(8,128)(2,1)S(1)} async-done(((bf16[16,64,128]{2,1,0:T(8,128)(2,1)}), bf16[16,64,128]{2,1,0:T(8,128)(2,1)S(1)}, u32[]{:S(2)}, u32[]{:S(2)}) %all-to-all-start.2) | async-done | bytes 262176 | tf_op jit(solution)/shard_map/all_to_all | solution.py:401
  58.0 2.3 %shard_map.60 = bf16[384,1024]{1,0:T(8,128)(2,1)S(1)} custom-call(s32[8,256]{1,0:T(8,128)S(1)} %get-tuple-element.29.place_ref, bf16[384,1024]{1,0:T(8,128)(2,1)S(1)} %copy-done.4, bf16[1024,128]{1,0:T(8,128)(2,1)S(1)} %bitcast.10, f32[384,1024]{1,0:T(8,128)S(1)} %get-tuple-element.31.mixed_ref, f32[48,128]{1,0:T(8,128)S(1)} %get-tuple-element.32.level_ref), custom_call_target="tpu_custom_call" | custom-call | flops 402653184 | bytes 3440640 | tf_op jit(solution)/shard_map/pallas_call | solution.py:336
  60.3 14.7 %all_to_all.46 = bf16[4,96,1024]{2,1,0:T(8,128)(2,1)S(1)} all-to-all(bf16[4,96,1024]{2,1,0:T(8,128)(2,1)S(1)} %bitcast.9), channel_id=1, replica_groups=mesh['ctx'=128,'kvh'=4] {'kvh'}, dimensions={0} | all-to-all | bytes 1572864 | tf_op jit(solution)/shard_map/all_to_all | solution.py:429
  75.0 0.9 %shard_map.61 = bf16[96,4096]{1,0:T(8,128)(2,1)} custom-call(bf16[384,1024]{1,0:T(8,128)(2,1)S(1)} %bitcast.8), custom_call_target="tpu_custom_call" | custom-call | bytes 1572864 | tf_op jit(solution)/shard_map/pallas_call | solution.py:336
Async XLA Ops:
  0.0 50.8 %copy-start.6 = (s32[2,4]{1,0:T(2,128)S(1)}, s32[2,4]{1,0:T(2,128)}, u32[]{:S(2)}) copy-start(s32[2,4]{1,0:T(2,128)} %vert_ref.2) | copy-start | bytes 100
  0.0 50.8 %copy-start.3 = (bf16[384,256]{1,0:T(8,128)(2,1)S(1)}, bf16[384,256]{1,0:T(8,128)(2,1)}, u32[]{:S(2)}) copy-start(bf16[384,256]{1,0:T(8,128)(2,1)} %v_ref.2) | copy-start | bytes 589828
  0.0 50.8 %copy-start.1 = (bf16[384,256]{1,0:T(8,128)(2,1)S(1)}, bf16[384,256]{1,0:T(8,128)(2,1)}, u32[]{:S(2)}) copy-start(bf16[384,256]{1,0:T(8,128)(2,1)} %k_ref.2) | copy-start | bytes 589828
  0.0 50.8 %copy-start.7 = (s32[2,3]{1,0:T(2,128)S(1)}, s32[2,3]{1,0:T(2,128)}, u32[]{:S(2)}) copy-start(s32[2,3]{1,0:T(2,128)} %off_ref.1) | copy-start | bytes 76
  1.8 16.1 %all-to-all-start = ((bf16[16,16,128]{2,1,0:T(8,128)(2,1)}), bf16[16,16,128]{2,1,0:T(8,128)(2,1)S(1)}, u32[]{:S(2)}, u32[]{:S(2)}) async-start(bf16[16,16,128]{2,1,0:T(8,128)(2,1)} %bitcast.13), calls=%async_computation | async-start | bytes 131072 | tf_op jit(solution)/shard_map/all_to_all | solution.py:379
  11.9 0.9 %copy-start = (bf16[384,256]{1,0:T(8,128)(2,1)S(1)}, bf16[384,256]{1,0:T(8,128)(2,1)}, u32[]{:S(2)}) copy-start(bf16[384,256]{1,0:T(8,128)(2,1)} %k_ref.2) | copy-start | bytes 589828
  12.9 0.9 %copy-start.2 = (bf16[384,256]{1,0:T(8,128)(2,1)S(1)}, bf16[384,256]{1,0:T(8,128)(2,1)}, u32[]{:S(2)}) copy-start(bf16[384,256]{1,0:T(8,128)(2,1)} %v_ref.2) | copy-start | bytes 589828
  13.8 0.7 copy-start.5
  14.5 36.4 %copy-start.4 = (bf16[384,1024]{1,0:T(8,128)(2,1)S(1)}, bf16[384,1024]{1,0:T(8,128)(2,1)}, u32[]{:S(2)}) copy-start(bf16[384,1024]{1,0:T(8,128)(2,1)} %q_ref.3) | copy-start | bytes 2359300
  18.6 24.3 %all-to-all-start.1 = ((bf16[8,64,128]{2,1,0:T(8,128)(2,1)}), bf16[8,64,128]{2,1,0:T(8,128)(2,1)S(1)}, u32[]{:S(2)}, u32[]{:S(2)}) async-start(bf16[8,64,128]{2,1,0:T(8,128)(2,1)} %bitcast.2), calls=%async_computation.1 | async-start | bytes 262144 | tf_op jit(solution)/shard_map/all_to_all | solution.py:391
  29.5 11.5 %collective-permute-start = (bf16[768,256]{1,0:T(8,128)(2,1)S(1)}, bf16[768,256]{1,0:T(8,128)(2,1)S(1)}, u32[]{:S(2)}, u32[]{:S(2)}) collective-permute-start(bf16[768,256]{1,0:T(8,128)(2,1)S(1)} %get-tuple-element.27), channel_id=1, source_target_pairs={{0,4},{4,8},{8,12},{12,16},{16,20},{20,24},{24,28},{28,32},{32,36}... | collective-permute-start | bytes 1179656 | tf_op jit(solution)/shard_map/ppermute | solution.py:390
  43.7 14.4 %all-to-all-start.2 = ((bf16[16,64,128]{2,1,0:T(8,128)(2,1)}), bf16[16,64,128]{2,1,0:T(8,128)(2,1)S(1)}, u32[]{:S(2)}, u32[]{:S(2)}) async-start(bf16[16,64,128]{2,1,0:T(8,128)(2,1)} %bitcast.4), calls=%async_computation.2 | async-start | bytes 524288 | tf_op jit(solution)/shard_map/all_to_all | solution.py:401
